TPU v7x, 32 devices: a whole 2x2x4 slice. The times are simulated.
32 devices in a mesh: leaf: 4 (over y, core), prow: 4 (over z), pcol: 2 (over x).
Axes of the slice: x: 2, y: 2, z: 4, core: 2. Of those that a mesh axis runs over, the one named last changes fastest.
Arguments:
- front_pivot: float32 [4, 1536, 1536], P('leaf', ('prow', 'pcol')), as said below
- front_lower: float32 [4, 6144, 1536], P('leaf', ('prow', 'pcol')), may hold values from -0.375 to 0.375
- front_rest: float32 [4, 6144, 6144], P('leaf', ('prow', 'pcol')), as said below
- parent_front: float32 [4, 8192, 4096], P('leaf', ('prow', 'pcol')), may hold values from -1.3 to 4.4, as said below
- relation: int32 [4, 6144], replicated, may hold values from 0 to 8191, as said below
Outputs:
- factor_pivot: float32 [4, 1536, 1536], P('leaf', ('prow', 'pcol'))
- factor_lower: float32 [4, 6144, 1536], P('leaf', ('prow', 'pcol'))
- parent_out: float32 [4, 8192, 4096], P('leaf', ('prow', 'pcol'))
Inputs may be any that keep to these rules, and one draw needn't show every extreme that they name: Each front_pivot[g] is symmetric positive definite, with no eigenvalue under 0.3. Each front_rest[g] is symmetric, with diagonal entries between 6 and 9 and small off-diagonal entries. `parent_front`: the two column halves of one parent front together form a symmetric matrix. `relation`: for every front and every k, the entries k * 768 to (k + 1) * 768 - 1 rise strictly and lie in k * 1024 to (k + 1) * 1024 - 1, and take both ends of that range.
All inputs are finite; a program needn't handle non-finite values.
Results may differ from a plain program's by a relative error of at most 0.0029.
Values may be sent and summed in bfloat16 or wider, within the bound.
No kernel may reach another device: no remote copies, remote signals or barrier semaphores. Data moves between devices by JAX's collectives and lax.ppermute only.
A program may use at most 192 MiB of HBM per device.

v0:
```python
import jax
import jax.numpy as jnp
from jax import lax
from jax.sharding import PartitionSpec as P

PW = 512


highest = lax.Precision.HIGHEST


def from_partner(value, axis, apart):
    mask = 2**apart
    pairs = [(source, source ^ mask) for source in range(lax.axis_size(axis))]
    return lax.ppermute(value, axis, pairs)


def factor_blocked(matrix):
    block_order = matrix.shape[0]
    if block_order <= 128:
        factor = jnp.linalg.cholesky(matrix)
        identity = jnp.eye(block_order, dtype=jnp.float32)
        inverse = lax.linalg.triangular_solve(factor, identity, left_side=True, lower=True)
        return (factor, inverse)
    middle = block_order // 2
    top_factor, top_inverse = factor_blocked(matrix[:middle, :middle])
    lower_block = jnp.dot(matrix[middle:, :middle], top_inverse.T, precision=highest)
    reduced = matrix[middle:, middle:] - jnp.dot(lower_block, lower_block.T, precision=highest)
    bottom_factor, bottom_inverse = factor_blocked(reduced)
    mixed_inverse = -jnp.dot(
        bottom_inverse, jnp.dot(lower_block, top_inverse, precision=highest), precision=highest
    )
    upper_zeros = jnp.zeros((middle, block_order - middle), jnp.float32)
    factor = jnp.concatenate(
        [
            jnp.concatenate([top_factor, upper_zeros], axis=1),
            jnp.concatenate([lower_block, bottom_factor], axis=1),
        ],
        axis=0,
    )
    inverse = jnp.concatenate(
        [
            jnp.concatenate([top_inverse, upper_zeros], axis=1),
            jnp.concatenate([mixed_inverse, bottom_inverse], axis=1),
        ],
        axis=0,
    )
    return (factor, inverse)


def local(front_pivot, front_lower, front_rest, parent_front, relation):
    position = lax.axis_index(("prow", "pcol"))
    pivot_rows = front_pivot[0]
    lower_rows = front_lower[0]
    pivot_order = pivot_rows.shape[1]
    rows_here = pivot_rows.shape[0]
    for panel_idx in range(pivot_order // PW):
        first_col = panel_idx * PW
        after_col = first_col + PW
        column = lax.all_gather(
            pivot_rows[:, first_col:after_col], ("prow", "pcol"), axis=0, tiled=True
        )
        corner, corner_inverse = factor_blocked(column[first_col:after_col])
        trailing = jnp.dot(column[after_col:], corner_inverse.T, precision=highest)
        full_panel = jnp.concatenate(
            [jnp.zeros((first_col, PW), jnp.float32), corner, trailing], axis=0
        )
        own_panel = lax.dynamic_slice_in_dim(full_panel, position * rows_here, rows_here, 0)
        lower_panel = jnp.dot(
            lower_rows[:, first_col:after_col], corner_inverse.T, precision=highest
        )
        pivot_rows = pivot_rows.at[:, first_col:after_col].set(own_panel)
        lower_rows = lower_rows.at[:, first_col:after_col].set(lower_panel)
        if after_col < pivot_order:
            pivot_rows = pivot_rows.at[:, after_col:].add(
                -jnp.dot(own_panel, trailing.T, precision=highest)
            )
            lower_rows = lower_rows.at[:, after_col:].add(
                -jnp.dot(lower_panel, trailing.T, precision=highest)
            )
    shared = lower_rows.astype(jnp.bfloat16)
    rest_rows = front_rest[0]
    block_rows = rest_rows.shape[0]
    child_order = rest_rows.shape[1]
    update = jnp.einsum(
        "ik,jk->ij",
        shared,
        lax.all_gather(shared, ("prow", "pcol"), axis=0, tiled=True),
        preferred_element_type=jnp.float32,
    )
    schur_rows = rest_rows - update
    leaf_index = lax.axis_index("leaf")
    side_bit = leaf_index % 2
    partner = leaf_index + 1 - 2 * side_bit
    child_half = child_order // 2
    window = parent_front.shape[1]
    parent_half = parent_front.shape[2]
    blocks = child_half // block_rows
    kept_cols = lax.dynamic_slice_in_dim(schur_rows, side_bit * child_half, child_half, 1)
    sent_cols = lax.dynamic_slice_in_dim(schur_rows, (1 - side_bit) * child_half, child_half, 1)
    received = from_partner(sent_cols.astype(jnp.bfloat16), "leaf", 0).astype(sent_cols.dtype)
    window_iota = jnp.arange(window, dtype=jnp.int32)
    block_starts = jnp.arange(blocks, dtype=jnp.int32) * window

    def spread(values, child_idx):
        link_map = lax.dynamic_index_in_dim(relation, child_idx, 0, keepdims=False)
        row_links = (
            lax.dynamic_slice_in_dim(link_map, position * block_rows, block_rows, 0)
            - position * window
        )
        col_links = (
            lax.dynamic_slice_in_dim(link_map, side_bit * child_half, child_half, 0)
            - side_bit * parent_half
        )
        col_local = col_links.reshape(blocks, block_rows) - block_starts[:, None]
        row_table = (window_iota[:, None] == row_links[None, :]).astype(jnp.float32)
        col_table = (col_local[:, :, None] == window_iota[None, None, :]).astype(jnp.float32)
        placed = jnp.einsum(
            "akb,kbj->akj",
            values.reshape(block_rows, blocks, block_rows),
            col_table,
            precision=highest,
        )
        return jnp.dot(row_table, placed.reshape(block_rows, blocks * window), precision=highest)

    merged = parent_front[0] + spread(kept_cols, leaf_index) + spread(received, partner)
    return (pivot_rows[None], lower_rows[None], merged[None])


def solution(mesh):
    return jax.shard_map(
        local,
        mesh=mesh,
        in_specs=(
            P("leaf", ("prow", "pcol"), None),
            P("leaf", ("prow", "pcol"), None),
            P("leaf", ("prow", "pcol"), None),
            P("leaf", ("prow", "pcol"), None),
            P(),
        ),
        out_specs=(
            P("leaf", ("prow", "pcol"), None),
            P("leaf", ("prow", "pcol"), None),
            P("leaf", ("prow", "pcol"), None),
        ),
        check_vma=False,
    )
```

profile of v0, /device:TPU:9, one launch (start us, length us, event | category | flops | bytes accessed | tf_op | source)
XLA Modules:
  0.0 1053.8 jit_solution(6879268388623583289)
XLA Ops:
  15.9 58.7 %all-gather.5.cloned.1.call-done = f32[1536,512]{1,0:T(8,128)} async-done(((f32[192,512]{1,0:T(8,128)}), f32[1536,512]{1,0:T(8,128)}) %all-gather.5.cloned.1.call-update) | async-done | bytes 3145744 | tf_op jit(solution)/shard_map/all_gather | solution.py:60
  76.4 11.7 %cholesky.194 = f32[128,128]{1,0:T(8,128)S(1)} custom-call(f32[128,128]{1,0:T(8,128)S(1)} %get-tuple-element.168), custom_call_target="Cholesky" | custom-call | tf_op jit(solution)/shard_map/jit(cholesky)/cholesky | solution.py:21
  89.5 9.8 custom-call.16
  101.6 11.7 %cholesky.205 = f32[128,128]{1,0:T(8,128)S(1)} custom-call(f32[128,128]{1,0:T(8,128)S(1)} %fusion.143), custom_call_target="Cholesky" | custom-call | tf_op jit(solution)/shard_map/jit(cholesky)/cholesky | solution.py:21
  114.7 10.0 custom-call.17
  129.3 11.7 %cholesky.216 = f32[128,128]{1,0:T(8,128)S(1)} custom-call(f32[128,128]{1,0:T(8,128)S(1)} %fusion.141), custom_call_target="Cholesky" | custom-call | tf_op jit(solution)/shard_map/jit(cholesky)/cholesky | solution.py:21
  142.4 9.8 custom-call.18
  154.4 12.1 %cholesky.227 = f32[128,128]{1,0:T(8,128)S(1)} custom-call(f32[128,128]{1,0:T(8,128)S(1)} %fusion.139), custom_call_target="Cholesky" | custom-call | tf_op jit(solution)/shard_map/jit(cholesky)/cholesky | solution.py:21
  167.8 9.8 custom-call.19
  198.2 55.6 %all-gather.7.cloned.1.call-done = f32[1536,512]{1,0:T(8,128)} async-done(((f32[192,512]{1,0:T(8,128)}), f32[1536,512]{1,0:T(8,128)}) %all-gather.7.cloned.1.call-update) | async-done | bytes 3145744 | tf_op jit(solution)/shard_map/all_gather | solution.py:60
  255.7 11.7 %cholesky.238 = f32[128,128]{1,0:T(8,128)S(1)} custom-call(f32[128,128]{1,0:T(8,128)S(1)} %get-tuple-element.166), custom_call_target="Cholesky" | custom-call | tf_op jit(solution)/shard_map/jit(cholesky)/cholesky | solution.py:21
  281.9 11.7 %cholesky.249 = f32[128,128]{1,0:T(8,128)S(1)} custom-call(f32[128,128]{1,0:T(8,128)S(1)} %fusion.135), custom_call_target="Cholesky" | custom-call | tf_op jit(solution)/shard_map/jit(cholesky)/cholesky | solution.py:21
  295.7 10.2 custom-call.21
  311.2 11.7 %cholesky.260 = f32[128,128]{1,0:T(8,128)S(1)} custom-call(f32[128,128]{1,0:T(8,128)S(1)} %fusion.133), custom_call_target="Cholesky" | custom-call | tf_op jit(solution)/shard_map/jit(cholesky)/cholesky | solution.py:21
  324.4 9.8 custom-call.22
  336.2 11.9 %cholesky.271 = f32[128,128]{1,0:T(8,128)S(1)} custom-call(f32[128,128]{1,0:T(8,128)S(1)} %fusion.131), custom_call_target="Cholesky" | custom-call | tf_op jit(solution)/shard_map/jit(cholesky)/cholesky | solution.py:21
  350.2 9.8 custom-call.23
  403.8 27.3 %all-gather.9.cloned.1.call-done = f32[1536,512]{1,0:T(8,128)} async-done(((f32[192,512]{1,0:T(8,128)}), f32[1536,512]{1,0:T(8,128)}) %all-gather.9.cloned.1.call-update) | async-done | bytes 3145744 | tf_op jit(solution)/shard_map/all_gather | solution.py:60
  433.1 11.7 %cholesky.282 = f32[128,128]{1,0:T(8,128)S(1)} custom-call(f32[128,128]{1,0:T(8,128)S(1)} %get-tuple-element.164), custom_call_target="Cholesky" | custom-call | tf_op jit(solution)/shard_map/jit(cholesky)/cholesky | solution.py:21
  446.1 9.8 custom-call.24
  458.2 11.7 %cholesky.293 = f32[128,128]{1,0:T(8,128)S(1)} custom-call(f32[128,128]{1,0:T(8,128)S(1)} %fusion.127), custom_call_target="Cholesky" | custom-call | tf_op jit(solution)/shard_map/jit(cholesky)/cholesky | solution.py:21
  471.3 9.8 custom-call.25
  484.9 11.7 %cholesky.304 = f32[128,128]{1,0:T(8,128)S(1)} custom-call(f32[128,128]{1,0:T(8,128)S(1)} %fusion.125), custom_call_target="Cholesky" | custom-call | tf_op jit(solution)/shard_map/jit(cholesky)/cholesky | solution.py:21
  498.0 10.0 custom-call.26
  509.9 11.7 %cholesky.315 = f32[128,128]{1,0:T(8,128)S(1)} custom-call(f32[128,128]{1,0:T(8,128)S(1)} %fusion.123), custom_call_target="Cholesky" | custom-call | tf_op jit(solution)/shard_map/jit(cholesky)/cholesky | solution.py:21
  522.9 9.8 custom-call.27
  542.1 362.7 %all-gather.11.cloned.1.call-done = bf16[6144,1536]{1,0:T(8,128)(2,1)} async-done(((bf16[768,1536]{1,0:T(8,128)(2,1)}), bf16[6144,1536]{1,0:T(8,128)(2,1)}) %all-gather.11.cloned.1.call-update) | async-done | bytes 18874384 | tf_op jit(solution)/shard_map/all_gather | solution.py:88
  904.8 26.9 %bitcast_subtract_fusion = f32[768,6144]{1,0:T(8,128)} fusion(f32[1,768,6144]{2,1,0:T(8,128)} %param.30, bf16[768,1536]{1,0:T(8,128)(2,1)} %convert_element_type.48, bf16[6144,1536]{1,0:T(8,128)(2,1)} %all-gather.11.cloned.1.call-done), kind=kOutput, calls=%fused_computation | convolution fusion | flops 14500233216 | bytes 58982400 | tf_op jit(solution)/shard_map/ik,jk->ij/dot_general | solution.py:85
  960.8 17.9 %fusion.2 = f32[4,1024,768]{2,1,0:T(8,128)S(1)} fusion(f32[768,4,768]{0,2,1:T(8,128)} %bitcast.224, s32[4,768]{1,0:T(4,128)S(1)} %get-tuple-element.170), kind=kOutput, calls=%fused_computation.6 | convolution fusion | flops 28994174976 | bytes 22032384 | tf_op jit(solution)/shard_map/akb,kbj->akj/dot_general | solution.py:118
  978.7 22.9 %fusion.8 = f32[1024,4096]{1,0:T(8,128)} fusion(f32[768,4096]{0,1:T(8,128)S(1)} %bitcast.227, s32[768]{0:T(1024)S(1)} %get-tuple-element.132), kind=kOutput, calls=%fused_computation.35 | convolution fusion | flops 38655492096 | bytes 29363200 | tf_op jit(solution)/shard_map/dot_general | solution.py:124
  1001.6 10.4 fusion.3
  1012.0 35.1 %fusion.1 = f32[1,1024,4096]{2,1,0:T(8,128)} fusion(f32[1024,4096]{1,0:T(8,128)} %fusion.8, f32[1,1024,4096]{2,1,0:T(8,128)} %param.31, f32[768,4096]{0,1:T(8,128)} %bitcast.223, s32[768]{0:T(1024)S(1)} %get-tuple-element.131), kind=kOutput, calls=%fused_computation.3 | convolution fusion | flops 38663880704 | bytes 62917632 | tf_op jit(solution)/shard_map/dot_general | solution.py:124
  (256 shorter events, 171.4 us)
Async XLA Ops:
  7.2 67.4 %all-gather.5.cloned.1.call-start = ((), (), s32[]{:S(2)}) async-start(), calls=%async_computation | async-start | bytes 3538944 | tf_op jit(solution)/shard_map/all_gather | solution.py:60
  14.1 239.7 %all-gather.7.cloned.1.call-start = ((), (), s32[]{:S(2)}) async-start(), calls=%async_computation.1 | async-start | bytes 3538944 | tf_op jit(solution)/shard_map/all_gather | solution.py:60
  178.0 1.4 copy-start.14
  178.3 1.1 copy-start.13
  178.3 1.1 copy-start.8
  179.4 5.8 copy-start.10
  179.4 5.8 copy-start.11
  179.4 5.8 copy-start.15
  179.8 7.5 copy-start.7
  185.2 7.7 copy-start
  192.9 0.9 copy-start.4
  194.6 236.5 %all-gather.9.cloned.1.call-start = ((), (), s32[]{:S(2)}) async-start(), calls=%async_computation.2 | async-start | bytes 3538944 | tf_op jit(solution)/shard_map/all_gather | solution.py:60
  336.1 30.6 %copy-start.16 = (f32[128,256]{1,0:T(8,128)}, f32[128,256]{1,0:T(8,128)S(1)}, u32[]{:S(2)}) copy-start(f32[128,256]{1,0:T(8,128)S(1)} %concatenate.212) | copy-start | bytes 393220
  336.1 30.6 %copy-start.5 = (f32[192,1024]{1,0:T(8,128)S(1)}, f32[192,1024]{1,0:T(8,128)}, u32[]{:S(2)}) copy-start(f32[192,1024]{1,0:T(8,128)} %copy-done.4) | copy-start | bytes 2359300
  361.0 5.8 copy-start.22
  361.2 7.5 copy-start.20
  363.4 3.3 copy-start.18
  366.7 4.2 copy-start.2
  368.8 3.1 slice-start
  370.8 1.0 copy-start.12
  371.9 0.9 copy-start.9
  371.9 532.9 %all-gather.11.cloned.1.call-start = ((), (), s32[]{:S(2)}) async-start(), calls=%async_computation.3 | async-start | bytes 21233664 | tf_op jit(solution)/shard_map/all_gather | solution.py:88
  379.5 6.1 copy-start.1
  382.7 2.8 copy-start.6
  385.5 8.5 copy-start.17
  385.5 8.5 copy-start.19
  385.5 8.5 copy-start.21
  385.6 8.5 copy-start.23
  385.6 8.5 copy-start.24
  394.0 4.5 copy-start.3
  938.3 63.3 %collective-permute-start = (bf16[768,3072]{1,0:T(8,128)(2,1)}, bf16[768,3072]{1,0:T(8,128)(2,1)}, u32[]{:S(2)}, u32[]{:S(2)}) collective-permute-start(bf16[768,3072]{1,0:T(8,128)(2,1)} %dynamic-slice_convert_fusion), channel_id=1, source_target_pairs={{0,8},{8,0},{16,24},{24,16},{1,9},{9,1},{17,25},{25,17},{2,10},{10... | collective-permute-start | bytes 14155784 | tf_op jit(solution)/shard_map/ppermute | solution.py:15
Sparse Core Ops, SparseCore 0:
  14.2 60.3 all-gather.4
  194.7 59.0 all-gather.6
  372.0 59.0 all-gather.8
  542.2 362.5 all-gather.10
where the time goes:
time: 1070 us; the launch traced here: 1050 us
  waiting for transfers between devices  504 us (47%)
  other arithmetic  297 us (28%)
  matrix products  177 us (17%)
  local copies, waits for them, and re-layouts  59.3 us (6%)
  between operations  15.4 us (1%)
    all_gather x1, waiting for transfers between devices, local(): lax.all_gather(shared, ('prow', 'pcol'), axis=0, tiled=True)  363 us
    another operation x36, other arithmetic, factor_blocked(): factor = jnp.linalg.cholesky(matrix)  149 us
    all_gather x3, waiting for transfers between devices, local(): lax.all_gather(pivot_rows[:, first_col:after_col], ('prow', 'pcol'), axis...  142 us
    another operation x24, other arithmetic, factor_blocked(): lax.linalg.triangular_solve(factor, identity, left_side=True, lower=True)  128 us
    dot_general x2, matrix products, spread(): jnp.dot(row_table, placed.reshape(block_rows, blocks * window), precision...  58 us
    dot_general x2, matrix products, spread(): jnp.einsum('akb,kbj->akj', values.reshape(block_rows, blocks, block_rows)...  28.2 us
    dot_general x1, matrix products, local(): jnp.einsum('ik,jk->ij', shared, lax.all_gather(shared, ('prow', 'pcol'),...  26.9 us
  transfers between devices with their start and end apart: 5, of which 4 were waited for; matrix products, arithmetic and copies ran while one was open for 9% of the time, Pallas kernels for 0%

commit v1 on v0

v1 whole, which is shorter than its diff:
```python
import math

import jax
import jax.numpy as jnp
from jax import lax
from jax.experimental import pallas as pl
from jax.experimental.pallas import tpu as pltpu
from jax.sharding import PartitionSpec as P

ROWS = ("prow", "pcol")
bf16 = jnp.bfloat16
f32 = jnp.float32
LANES = 128
SUBS = 8
VMEM_LIMIT = 56 << 20


def panel_widths(order):
    narrow = order // 6
    return (narrow, 2 * narrow, 2 * narrow, narrow)


def split(x):
    top = x.astype(bf16)
    return top, (x - top.astype(f32)).astype(bf16)


def left_parts(x):
    top, low = split(x)
    return jnp.concatenate([top, top, low], axis=1)


def right_parts(x):
    top, low = split(x)
    return jnp.concatenate([top, low, top], axis=1)


def nt(a, b):
    return lax.dot_general(a, b, (((1,), (1,)), ((), ())), preferred_element_type=f32)


def nn(a, b):
    return jnp.dot(a, b, preferred_element_type=f32)


def spread_lane(x, lane):
    return jnp.broadcast_to(x[:, lane:lane + 1], (SUBS, LANES))


def spread_sub(x, sub):
    return jnp.broadcast_to(x[sub:sub + 1, :], (SUBS, LANES))


def factor_square(square):
    lane = lax.broadcasted_iota(jnp.int32, (SUBS, LANES), 1)
    sub = lax.broadcasted_iota(jnp.int32, (SUBS, LANES), 0)
    count = LANES // SUBS
    state = [square[SUBS * r:SUBS * (r + 1), :] for r in range(count)]
    uppers, inverses = [], []
    for b in range(count):
        first = SUBS * b
        block = state[b]
        inside = (lane >= first) & (lane < first + SUBS)
        columns = [spread_lane(block, first + k) for k in range(SUBS)]
        d = [
            [spread_sub(columns[k], i) if k >= i else None for k in range(SUBS)]
            for i in range(SUBS)
        ]
        packed = jnp.where(inside, (lane - first == sub).astype(f32), block)
        corner = jnp.where(inside, block, 0.0)
        rows = [spread_sub(packed, i) for i in range(SUBS)]
        corners = [spread_sub(corner, i) for i in range(SUBS)]
        follow = b + 1 < count
        if follow:
            ahead = state[b + 1]
            beside = [spread_lane(ahead, first + k) for k in range(SUBS)]
            ahead = jnp.where(inside, 0.0, ahead)
        scales, steps = [], []
        for i in range(SUBS):
            scale = lax.rsqrt(d[i][i])
            scales.append(scale)
            rows[i] = rows[i] * scale
            corners[i] = corners[i] * scale
            step = [d[i][k] * scale if k > i else None for k in range(SUBS)]
            steps.append(step)
            if follow:
                beside[i] = beside[i] * scale
                ahead = ahead - beside[i] * rows[i]
            for k in range(i + 1, SUBS):
                for m in range(k, SUBS):
                    d[k][m] = d[k][m] - step[k] * step[m]
                rows[k] = rows[k] - step[k] * rows[i]
                corners[k] = corners[k] - step[k] * corners[i]
                if follow:
                    beside[k] = beside[k] - step[k] * beside[i]
        whole, whole_corner = rows[0], corners[0]
        for i in range(1, SUBS):
            whole = jnp.where(sub == i, rows[i], whole)
            whole_corner = jnp.where(sub == i, corners[i], whole_corner)
        inverses.append(jnp.where(lane < first + SUBS, whole, 0.0))
        upper = jnp.where(lane >= first + SUBS, whole, whole_corner)
        uppers.append(jnp.where(lane >= first + sub, upper, 0.0))
        if follow:
            state[b + 1] = ahead
        if b + 2 < count:
            back = [None] * SUBS
            for i in reversed(range(SUBS)):
                total = rows[i]
                for k in range(i + 1, SUBS):
                    total = total - steps[i][k] * back[k]
                back[i] = total * scales[i]
            for r in range(b + 2, count):
                below = state[r]
                left = [spread_lane(below, first + k) for k in range(SUBS)]
                below = jnp.where(inside, 0.0, below)
                for k in range(SUBS):
                    below = below - left[k] * back[k]
                state[r] = below
    return jnp.concatenate(uppers, axis=0), jnp.concatenate(inverses, axis=0)


def largest_tile(rows):
    return next(t for t in (256, 128, 64, 32, 16, 8) if rows % t == 0)


def panel_kernel(before, *refs):
    pivot_in, lower_in = refs[:2]
    earlier = [(refs[2 + 2 * q], refs[3 + 2 * q]) for q in range(before)]
    pivot, lower, rounded, tops = refs[2 + 2 * before:6 + 2 * before]
    crowns = refs[6 + 2 * before:]
    width = pivot.shape[1]
    count = width // LANES
    pivot_rest = pivot.shape[0] - width
    starts = [past.shape[0] - pivot.shape[0] for past, _ in earlier]
    for q in range(before):
        for t in range(count):
            crowns[q][t * LANES:(t + 1) * LANES, :] = right_parts(
                earlier[q][0][starts[q] + t * LANES:starts[q] + (t + 1) * LANES, :]
            )

    def load(source, target, pasts, offsets):
        tile = largest_tile(source.shape[0])

        @pl.loop(0, source.shape[0] // tile)
        def _(t):
            first = pl.multiple_of(t * tile, tile)
            values = source[pl.ds(first, tile), :]
            for q in range(before):
                past = pasts[q][pl.ds(pl.multiple_of(offsets[q] + first, 8), tile), :]
                values = values - nt(left_parts(past), crowns[q][...])
            target[pl.ds(first, tile), :] = values

    load(pivot_in, pivot, [past for past, _ in earlier], starts)
    load(lower_in, lower, [past for _, past in earlier], [0] * before)

    @pl.loop(0, count)
    def _(k):
        here = pl.ds(pl.multiple_of(k * LANES, LANES), LANES)
        upper, inverse = factor_square(pivot[here, here])
        pivot[here, here] = upper.T
        solver = right_parts(inverse)
        for t in range(count):
            block = slice(t * LANES, (t + 1) * LANES)

            @pl.when(t < k)
            def _():
                pivot[block, here] = jnp.zeros((LANES, LANES), f32)

            @pl.when(t > k)
            def _():
                solved = nt(left_parts(pivot[block, here]), solver)
                pivot[block, here] = solved
                tops[block, :] = right_parts(solved)

        for c in range(1, count):
            cols = slice(c * LANES, (c + 1) * LANES)

            @pl.when(c > k)
            def _():
                solved = left_parts(pivot[c * LANES:width, here])
                pivot[c * LANES:width, cols] -= nt(solved, tops[cols, :])

        def run(ref, start, rows):
            tile = largest_tile(rows)

            @pl.loop(0, rows // tile)
            def _(t):
                band = pl.ds(pl.multiple_of(start + t * tile, 8), tile)
                solved = nt(left_parts(ref[band, here]), solver)
                ref[band, here] = solved
                parts = left_parts(solved)
                for c in range(1, count):
                    cols = slice(c * LANES, (c + 1) * LANES)

                    @pl.when(c > k)
                    def _():
                        ref[band, cols] -= nt(parts, tops[cols, :])

        if pivot_rest:
            run(pivot, width, pivot_rest)
        run(lower, 0, lower.shape[0])

    tile = largest_tile(lower.shape[0])

    @pl.loop(0, lower.shape[0] // tile)
    def _(t):
        here = pl.ds(pl.multiple_of(t * tile, tile), tile)
        rounded[here, :] = lower[here, :].astype(bf16)


def factor_panel(column, lower, earlier):
    width = column.shape[1]
    before = len(earlier)
    flat = [past for pair in earlier for past in pair]
    return pl.pallas_call(
        lambda *refs: panel_kernel(before, *refs),
        out_shape=(
            jax.ShapeDtypeStruct(column.shape, f32),
            jax.ShapeDtypeStruct(lower.shape, f32),
            jax.ShapeDtypeStruct(lower.shape, bf16),
        ),
        in_specs=[pl.BlockSpec(memory_space=pltpu.VMEM)] * (2 + len(flat)),
        out_specs=[pl.BlockSpec(memory_space=pltpu.VMEM)] * 3,
        scratch_shapes=[pltpu.VMEM((width, 3 * LANES), bf16)]
        + [pltpu.VMEM((width, 3 * past.shape[1]), bf16) for past, _ in earlier],
        compiler_params=pltpu.CompilerParams(vmem_limit_bytes=VMEM_LIMIT),
        cost_estimate=pl.CostEstimate(
            flops=width * 50000000, bytes_accessed=10 * (column.size + lower.size), transcendentals=0
        ),
    )(column, lower, *flat)


def one_hot(links, window):
    places = lax.broadcasted_iota(jnp.int32, (window, links.shape[1]), 0)
    return (places == links).astype(bf16)


def rest_kernel(side, own, other, own_rows, other_rows, own_cols, other_cols, parent, out, table, placed):
    window = out.shape[0]
    rows = own.shape[0]
    for source, (values, row_links, col_links) in enumerate(
        ((own, own_rows, own_cols), (other, other_rows, other_cols))
    ):
        first = 2 * source * rows

        @pl.when(pl.program_id(0) == 0)
        def _():
            spread = one_hot(row_links[0], window)
            table[:, first:first + rows] = spread
            table[:, first + rows:first + 2 * rows] = spread

        top, low = split(values[...])
        for i in range(col_links.shape[0]):
            spread = one_hot(col_links[i, 0], window)
            block, area = slice(i * rows, (i + 1) * rows), slice(i * window, (i + 1) * window)
            placed[first:first + rows, area] = nt(top[:, block], spread).astype(bf16)
            placed[first + rows:first + 2 * rows, area] = nt(low[:, block], spread).astype(bf16)
    tile = largest_tile(window)

    @pl.loop(0, window // tile)
    def _(t):
        here = pl.ds(pl.multiple_of(t * tile, tile), tile)
        out[here, :] = parent[here, :] + nn(table[here, :], placed[...])


def add_rest(parent, rest, received, side, row_links, col_links):
    window = parent.shape[0]
    rows = rest.shape[0]
    group = LANES // math.gcd(LANES, rows)
    steps = parent.shape[1] // window // group
    links = [pl.BlockSpec((1, 1, rows), lambda w, side: (0, 0, 0))] * 2 + [
        pl.BlockSpec((group, 1, 1, rows), lambda w, side: (w, 0, 0, 0))
    ] * 2
    area = pl.BlockSpec((window, group * window), lambda w, side: (0, w))
    return pl.pallas_call(
        rest_kernel,
        out_shape=jax.ShapeDtypeStruct(parent.shape, f32),
        grid_spec=pltpu.PrefetchScalarGridSpec(
            num_scalar_prefetch=1,
            grid=(steps,),
            in_specs=[
                pl.BlockSpec((rows, group * rows), lambda w, side: (0, side[0] * steps + w)),
                pl.BlockSpec((rows, group * rows), lambda w, side: (0, w)),
            ]
            + links
            + [area],
            out_specs=area,
            scratch_shapes=[
                pltpu.VMEM((window, 4 * rows), bf16),
                pltpu.VMEM((4 * rows, group * window), bf16),
            ],
        ),
        compiler_params=pltpu.CompilerParams(vmem_limit_bytes=VMEM_LIMIT),
        cost_estimate=pl.CostEstimate(
            flops=8 * rows * parent.size + 8 * rows * rows * parent.shape[1],
            bytes_accessed=8 * parent.size + 8 * received.size,
            transcendentals=0,
        ),
    )(side, rest, received, *row_links, *col_links, parent)


def rows_kernel(own, other, own_links, other_links, out):
    window, width = out.shape[0], own.shape[1]
    for source, (values, links) in enumerate(((own, own_links), (other, other_links))):
        out[:, source * width:(source + 1) * width] = nn(
            one_hot(links[0], window), values[...]
        ).astype(bf16)


def spread_rows(own, other, row_links, window):
    return pl.pallas_call(
        rows_kernel,
        out_shape=jax.ShapeDtypeStruct((window, 2 * own.shape[1]), bf16),
        compiler_params=pltpu.CompilerParams(vmem_limit_bytes=VMEM_LIMIT),
        cost_estimate=pl.CostEstimate(
            flops=4 * window * own.size, bytes_accessed=12 * own.size, transcendentals=0
        ),
    )(own, other, *row_links)


def update_kernel(places, rows, own, other, own_links, other_links, total, out, cols):
    window, width = out.shape[0], own.shape[2]
    for source, (values, links) in enumerate(((own, own_links), (other, other_links))):
        cols[:, source * width:(source + 1) * width] = nn(
            one_hot(links[0, 0], window), values[0]
        ).astype(bf16)
    tile = largest_tile(window)

    @pl.loop(0, window // tile)
    def _(t):
        here = pl.ds(pl.multiple_of(t * tile, tile), tile)
        out[here, :] = total[here, :] - nt(rows[here, :], cols[...])


def update_windows(total, rows, own, other, places, col_links):
    window = total.shape[0]
    count, children, width = own.shape
    block = pl.BlockSpec((1, children, width), lambda i, places: (i, 0, 0))
    link = pl.BlockSpec((1, 1, 1, children), lambda i, places: (places[i], 0, 0, 0))
    area = pl.BlockSpec((window, window), lambda i, places: (0, places[i]))
    return pl.pallas_call(
        update_kernel,
        out_shape=jax.ShapeDtypeStruct(total.shape, f32),
        grid_spec=pltpu.PrefetchScalarGridSpec(
            num_scalar_prefetch=1,
            grid=(count,),
            in_specs=[
                pl.BlockSpec((window, 2 * width), lambda i, places: (0, 0)),
                block,
                block,
                link,
                link,
                area,
            ],
            out_specs=area,
            scratch_shapes=[pltpu.VMEM((window, 2 * width), bf16)],
        ),
        input_output_aliases={6: 0},
        compiler_params=pltpu.CompilerParams(vmem_limit_bytes=VMEM_LIMIT),
        cost_estimate=pl.CostEstimate(
            flops=4 * count * window * width * (window + children),
            bytes_accessed=8 * count * window * window,
            transcendentals=0,
        ),
    )(places, rows, own, other, *col_links, total)


def local(front_pivot, front_lower, front_rest, parent_front, relation):
    leaves, prows, pcols = (lax.axis_size(a) for a in ("leaf", "prow", "pcol"))
    position = lax.axis_index(ROWS)
    here, across = lax.axis_index("prow"), lax.axis_index("pcol")
    pivot_rows, lower_rows = front_pivot[0], front_lower[0]
    rest_rows, parent_rows = front_rest[0], parent_front[0]
    rows_here, pivot_order = pivot_rows.shape
    block_rows, child_order = rest_rows.shape
    window = parent_rows.shape[0]
    child_half = child_order // 2
    blocks = child_half // block_rows
    near = prows // 2
    leaf_index = lax.axis_index("leaf")
    side = leaf_index % 2
    partner = leaf_index + 1 - 2 * side

    def to_sibling(value):
        return lax.ppermute(value, "leaf", [(g, g ^ 1) for g in range(leaves)])

    def to_cols(value, apart, swap):
        pairs = [
            ((g * prows + r) * pcols + c, ((g ^ swap) * prows + r) * pcols + (c + apart) % pcols)
            for g in range(leaves)
            for r in range(prows)
            for c in range(pcols)
        ]
        return lax.ppermute(value, ("leaf",) + ROWS, pairs)

    def links_of(child):
        links = lax.dynamic_index_in_dim(relation, child, 0, keepdims=False)
        rows = lax.dynamic_slice_in_dim(links, position * block_rows, block_rows, 0)
        cols = lax.dynamic_slice_in_dim(links, side * child_half, child_half, 0)
        cols = cols.reshape(blocks, 1, 1, block_rows)
        first = side * blocks + jnp.arange(blocks, dtype=jnp.int32)
        return (
            (rows - position * window).reshape(1, 1, block_rows),
            cols - first.reshape(blocks, 1, 1, 1) * window,
        )

    own_row_links, own_col_links = links_of(leaf_index)
    other_row_links, other_col_links = links_of(partner)
    row_links = (own_row_links, other_row_links)
    col_links = (own_col_links, other_col_links)

    widths = panel_widths(pivot_order)
    starts = [sum(widths[:p]) for p in range(len(widths))]
    columns = [
        lax.all_gather(pivot_rows[:, s:s + w], ROWS, axis=0, tiled=True)
        for s, w in zip(starts, widths)
    ]

    leaving = lax.dynamic_slice_in_dim(rest_rows, (1 - side) * child_half, child_half, 1)
    total = add_rest(
        parent_rows,
        rest_rows,
        to_sibling(leaving),
        side.astype(jnp.int32).reshape(1),
        row_links,
        col_links,
    )

    done, panels = [], []
    for s, w, column in zip(starts, widths, columns):
        pivot, lower, rounded = factor_panel(column[s:], lower_rows[:, s:s + w], done)
        done.append((pivot, lower))
        other = to_sibling(rounded)
        ring = [rounded] + [
            lax.ppermute(rounded, "prow", [(r, (r + step) % prows) for r in range(prows)])
            for step in range(1, prows)
        ]
        ring = jnp.stack(ring)

        def half(which):
            first = which * near
            return jnp.stack(
                [
                    lax.dynamic_index_in_dim(
                        ring, lax.rem(here - first - i + prows, prows), 0, keepdims=False
                    )
                    for i in range(near)
                ]
            )

        kept, sent = half(side), half(1 - side)
        panels.append((rounded, other, kept, sent))

    for rounded, other, kept, sent in panels:
        rows = spread_rows(rounded, other, row_links, window)
        for apart in range(pcols):
            own = to_cols(kept, apart, 0) if apart else kept
            sibling = to_cols(sent, apart, 1)
            places = jnp.arange(near, dtype=jnp.int32) * pcols + lax.rem(
                across - apart + pcols, pcols
            ).astype(jnp.int32)
            total = update_windows(total, rows, own, sibling, places, col_links)

    factor_rows = jnp.concatenate(
        [
            lax.dynamic_slice_in_dim(
                jnp.concatenate([jnp.zeros((s, w), f32), pivot], axis=0),
                position * rows_here,
                rows_here,
                0,
            )
            for s, w, (pivot, _) in zip(starts, widths, done)
        ],
        axis=1,
    )
    lower_out = jnp.concatenate([lower for _, lower in done], axis=1)
    return (factor_rows[None], lower_out[None], total[None])


def solution(mesh):
    whole = P("leaf", ROWS, None)
    return jax.shard_map(
        local,
        mesh=mesh,
        in_specs=(whole, whole, whole, whole, P()),
        out_specs=(whole, whole, whole),
        check_vma=False,
    )
```

time: 1070 us -> 753 us (0.70)
  Pallas kernels: 0 us -> 302 us
  other arithmetic: 297 us -> 15.8 us
  matrix products: 177 us -> 0 us
  waiting for transfers between devices: 504 us -> 351 us
  starting transfers between devices: 0.62 us -> 33 us
  local copies, waits for them, and re-layouts: 59.3 us -> 30.5 us
    all_gather x4, waiting for transfers between devices: 504 us -> 181 us  [local(): lax.all_gather(pivot_rows[:, s:s + w], ROWS, axis=0, tiled=True)]
    pallas_call x0 -> x17, Pallas kernels: none -> 302 us  [the longest x4 120 us: factor_panel(): pl.pallas_call(lambda *refs: panel_kernel(before, *refs), out_shape=(jax....]
    another operation x63 -> x12, other arithmetic: 281 us -> 7.62 us  [the longest x8 3.9 us: half(): jnp.stack([lax.dynamic_index_in_dim(ring, lax.rem(here - first - i + prow...]
    dot_general x50 -> x0, matrix products: 174 us -> none  [the longest x2 58 us: spread(): jnp.dot(row_table, placed.reshape(block_rows, blocks * window), precision...]
    ppermute x1 -> x29, waiting for transfers between devices: 0.01 us -> 168 us  [the longest x12 139 us: local(): lax.ppermute(rounded, 'prow', [(r, (r + step) % prows) for r in range(pro...]
    ppermute x1 -> x29, starting transfers between devices: 0.46 us -> 32.8 us  [the longest x5 11.3 us: to_sibling(): return lax.ppermute(value, 'leaf', [(g, g ^ 1) for g in range(leaves)])]
  transfers between devices with their start and end apart: 5 -> 33, of which waited for: 4 -> 15; matrix products, arithmetic and copies ran while one was open for 9% -> 6% of each run, Pallas kernels for 0% -> 39%
where the time goes in v1:
time: 753 us; the launch traced here: 747 us
  waiting for transfers between devices  351 us (47%)
  Pallas kernels  302 us (40%)
  starting transfers between devices  33 us (4%)
  local copies, waits for them, and re-layouts  30.5 us (4%)
  other arithmetic  15.8 us (2%)
  between operations  14.6 us (2%)
    all_gather x4, waiting for transfers between devices, local(): lax.all_gather(pivot_rows[:, s:s + w], ROWS, axis=0, tiled=True)  181 us
    ppermute x12, waiting for transfers between devices, local(): lax.ppermute(rounded, 'prow', [(r, (r + step) % prows) for r in range(pro...  139 us
    pallas_call x4, Pallas kernels, factor_panel(): pl.pallas_call(lambda *refs: panel_kernel(before, *refs), out_shape=(jax....  120 us
    pallas_call x8, Pallas kernels, update_windows(): pl.pallas_call(update_kernel, out_shape=jax.ShapeDtypeStruct(total.shape,...  110 us
    pallas_call x1, Pallas kernels, add_rest(): pl.pallas_call(rest_kernel, out_shape=jax.ShapeDtypeStruct(parent.shape,...  56.8 us
    ppermute x12, waiting for transfers between devices, to_cols(): return lax.ppermute(value, ('leaf',) + ROWS, pairs)  29.3 us
    pallas_call x4, Pallas kernels, spread_rows(): pl.pallas_call(rows_kernel, out_shape=jax.ShapeDtypeStruct((window, 2 * o...  15.2 us
  transfers between devices with their start and end apart: 33, of which 15 were waited for; matrix products, arithmetic and copies ran while one was open for 6% of the time, Pallas kernels for 39%

profile of v1, /device:TPU:9, one launch (start us, length us, event | category | flops | bytes accessed | tf_op | source)
XLA Modules:
  0.0 747.0 jit_solution(5759949826261384897)
XLA Ops:
  11.5 8.6 %dynamic-slice_bitcast_fusion = f32[768,3072]{1,0:T(8,128)} fusion(f32[1,768,6144]{2,1,0:T(8,128)} %param.7, s32[]{:T(128)S(6)} %select_n.79), kind=kLoop, calls=%fused_computation | loop fusion | bytes 18874372 | tf_op jit(solution)/shard_map/dynamic_slice | solution.py:419
  26.4 4.0 fusion.2
  30.4 25.5 %all-gather.5.cloned.1.call-done.refs_0_ = f32[1536,256]{1,0:T(8,128)} async-done(((f32[192,256]{1,0:T(8,128)}), f32[1536,256]{1,0:T(8,128)}) %all-gather.5.cloned.1.call-update) | async-done | bytes 1572880 | tf_op jit(solution)/shard_map/all_gather | solution.py:415
  55.9 18.0 %shard_map.76 = (f32[1536,256]{1,0:T(8,128)}, f32[768,256]{1,0:T(8,128)}, bf16[768,256]{1,0:T(8,128)(2,1)}) custom-call(f32[1536,256]{1,0:T(8,128)} %all-gather.5.cloned.1.call-done.refs_0_, f32[768,256]{1,0:T(8,128)} %get-tuple-element.29.refs_1_), custom_call_target="tpu_custom_call" | custom-call | flops 12800000000 | bytes 5898240 | tf_op jit(solution)/shard_map/pallas_call | solution.py:215
  78.4 41.4 %all-gather.11.cloned.1.call-done = f32[1536,256]{1,0:T(8,128)} async-done(((f32[192,256]{1,0:T(8,128)}), f32[1536,256]{1,0:T(8,128)}) %all-gather.11.cloned.1.call-update) | async-done | bytes 1572880 | tf_op jit(solution)/shard_map/all_gather | solution.py:415
  126.6 56.7 %all-gather.7.cloned.1.call-done = f32[1536,512]{1,0:T(8,128)} async-done(((f32[192,512]{1,0:T(8,128)}), f32[1536,512]{1,0:T(8,128)}) %all-gather.7.cloned.1.call-update) | async-done | bytes 3145744 | tf_op jit(solution)/shard_map/all_gather | solution.py:415
  186.7 57.7 %all-gather.9.cloned.1.call-done = f32[1536,512]{1,0:T(8,128)} async-done(((f32[192,512]{1,0:T(8,128)}), f32[1536,512]{1,0:T(8,128)}) %all-gather.9.cloned.1.call-update) | async-done | bytes 3145744 | tf_op jit(solution)/shard_map/all_gather | solution.py:415
  247.1 42.7 %shard_map.77 = (f32[1280,512]{1,0:T(8,128)}, f32[768,512]{1,0:T(8,128)}, bf16[768,512]{1,0:T(8,128)(2,1)}) custom-call(f32[1280,512]{1,0:T(8,128)} %slice.47.refs_0_, f32[768,512]{1,0:T(8,128)} %get-tuple-element.28.refs_1_, f32[1536,256]{1,0:T(8,128)} %get-tuple-element.15.refs_2_, f32[768,256]{1,0:T(8,128)} %get-tuple-element.16.refs_3_), custom_call_target="tpu_custom_call" | custom-call | flops 25600000000 | bytes 10485760 | tf_op jit(solution)/shard_map/pallas_call | solution.py:215
  289.8 40.1 %shard_map.78 = (f32[768,512]{1,0:T(8,128)}, f32[768,512]{1,0:T(8,128)}, bf16[768,512]{1,0:T(8,128)(2,1)}) custom-call(f32[768,512]{1,0:T(8,128)} %slice.50.refs_0_, f32[768,512]{1,0:T(8,128)} %get-tuple-element.27.refs_1_, f32[1536,256]{1,0:T(8,128)} %get-tuple-element.15.refs_2_, f32[768,256]{1,0:T(8,128)} %get-tuple-element.16.refs_3_, ...), custom_call_target="tpu_custom_call" | custom-call | flops 25600000000 | bytes 7864320 | tf_op jit(solution)/shard_map/pallas_call | solution.py:215
  329.8 19.7 %shard_map.79 = (f32[256,256]{1,0:T(8,128)}, f32[768,256]{1,0:T(8,128)}, bf16[768,256]{1,0:T(8,128)(2,1)}) custom-call(f32[256,256]{1,0:T(8,128)} %slice.53.refs_0_, f32[768,256]{1,0:T(8,128)} %get-tuple-element.30.refs_1_, f32[1536,256]{1,0:T(8,128)} %get-tuple-element.15.refs_2_, f32[768,256]{1,0:T(8,128)} %get-tuple-element.16.refs_3_, ...), custom_call_target="tpu_custom_call" | custom-call | flops 12800000000 | bytes 2621440 | tf_op jit(solution)/shard_map/pallas_call | solution.py:215
  361.9 21.6 %collective-permute-done.2 = bf16[768,256]{1,0:T(8,128)(2,1)S(1)} collective-permute-done((bf16[768,256]{1,0:T(8,128)(2,1)}, bf16[768,256]{1,0:T(8,128)(2,1)S(1)}, u32[]{:S(2)}, u32[]{:S(2)}) %collective-permute-start.2) | collective-permute-done | bytes 393248 | tf_op jit(solution)/shard_map/ppermute | solution.py:435
  383.5 4.2 collective-permute-start
  388.8 32.0 %collective-permute-done.3 = bf16[768,256]{1,0:T(8,128)(2,1)S(1)} collective-permute-done((bf16[768,256]{1,0:T(8,128)(2,1)}, bf16[768,256]{1,0:T(8,128)(2,1)S(1)}, u32[]{:S(2)}, u32[]{:S(2)}) %collective-permute-start.3) | collective-permute-done | bytes 393248 | tf_op jit(solution)/shard_map/ppermute | solution.py:435
  425.9 8.2 %collective-permute-done.8 = bf16[768,512]{1,0:T(8,128)(2,1)S(1)} collective-permute-done((bf16[768,512]{1,0:T(8,128)(2,1)}, bf16[768,512]{1,0:T(8,128)(2,1)S(1)}, u32[]{:S(2)}, u32[]{:S(2)}) %collective-permute-start.8) | collective-permute-done | bytes 786464 | tf_op jit(solution)/shard_map/ppermute | solution.py:435
  434.1 33.7 %collective-permute-done.9 = bf16[768,512]{1,0:T(8,128)(2,1)S(1)} collective-permute-done((bf16[768,512]{1,0:T(8,128)(2,1)}, bf16[768,512]{1,0:T(8,128)(2,1)S(1)}, u32[]{:S(2)}, u32[]{:S(2)}) %collective-permute-start.9) | collective-permute-done | bytes 786464 | tf_op jit(solution)/shard_map/ppermute | solution.py:435
  470.0 18.4 %collective-permute-done.10 = bf16[768,512]{1,0:T(8,128)(2,1)} collective-permute-done((bf16[768,512]{1,0:T(8,128)(2,1)}, bf16[768,512]{1,0:T(8,128)(2,1)}, u32[]{:S(2)}, u32[]{:S(2)}) %collective-permute-start.10) | collective-permute-done | bytes 786464 | tf_op jit(solution)/shard_map/ppermute | solution.py:435
  491.0 10.5 %collective-permute-done.15 = bf16[768,512]{1,0:T(8,128)(2,1)} collective-permute-done((bf16[768,512]{1,0:T(8,128)(2,1)}, bf16[768,512]{1,0:T(8,128)(2,1)}, u32[]{:S(2)}, u32[]{:S(2)}) %collective-permute-start.15) | collective-permute-done | bytes 786464 | tf_op jit(solution)/shard_map/ppermute | solution.py:435
  501.5 4.2 collective-permute-start.7
  505.7 12.6 %collective-permute-done.16 = bf16[768,512]{1,0:T(8,128)(2,1)S(1)} collective-permute-done((bf16[768,512]{1,0:T(8,128)(2,1)}, bf16[768,512]{1,0:T(8,128)(2,1)S(1)}, u32[]{:S(2)}, u32[]{:S(2)}) %collective-permute-start.16) | collective-permute-done | bytes 786464 | tf_op jit(solution)/shard_map/ppermute | solution.py:435
  526.1 4.5 shard_map.82.rows
  532.0 4.5 shard_map.81.rows
  538.8 56.8 %shard_map.84.total = f32[1024,4096]{1,0:T(8,128)} custom-call(s32[1]{0:T(128)} %bitcast.24.side, f32[768,6144]{1,0:T(8,128)} %bitcast.37, f32[768,3072]{1,0:T(8,128)} %collective-permute-done.28.other, s32[1,1,768]{2,1,0:T(1,128)} %get-tuple-element.54.own_links.own_rows, s32[1,1,768]{2,1,0:T(1,128)} %get-tuple-element.53.other_links.other_rows, ...), custom_call_target="tpu_custom_call" | custom-call | flops 45097156608 | bytes 52428800 | tf_op jit(solution)/shard_map/pallas_call | solution.py:275
  595.5 11.7 %shard_map.85.total = f32[1024,4096]{1,0:T(8,128)} custom-call(s32[2]{0:T(128)} %fusion.places, bf16[1024,512]{1,0:T(8,128)(2,1)} %shard_map.83.rows, bf16[2,768,256]{2,1,0:T(8,128)(2,1)} %copy-done.3, bf16[2,768,256]{2,1,0:T(8,128)(2,1)} %collective-permute-done.27.other, ...), custom_call_target="tpu_custom_call", output_to_operand_aliasing={{}: (6, {})} | custom-call | flops 3758096384 | bytes 16777216 | tf_op jit(solution)/shard_map/pallas_call | solution.py:341
  608.4 11.5 %shard_map.86.total = f32[1024,4096]{1,0:T(8,128)} custom-call(s32[2]{0:T(128)} %fusion.1.places, bf16[1024,512]{1,0:T(8,128)(2,1)} %shard_map.83.rows, bf16[2,768,256]{2,1,0:T(8,128)(2,1)} %collective-permute-done.25.own, bf16[2,768,256]{2,1,0:T(8,128)(2,1)} %collective-permute-done.26.other, ...), custom_call_target="tpu_custom_call", output_to_operand_aliasing={{}: (6, {})} | custom-call | flops 3758096384 | bytes 16777216 | tf_op jit(solution)/shard_map/pallas_call | solution.py:341
  620.7 16.0 %shard_map.87.total = f32[1024,4096]{1,0:T(8,128)} custom-call(s32[2]{0:T(128)} %fusion.places, bf16[1024,1024]{1,0:T(8,128)(2,1)} %shard_map.82.rows, bf16[2,768,512]{2,1,0:T(8,128)(2,1)} %copy-done.1, bf16[2,768,512]{2,1,0:T(8,128)(2,1)} %collective-permute-done.20.other, ...), custom_call_target="tpu_custom_call", output_to_operand_aliasing={{}: (6, {})} | custom-call | flops 7516192768 | bytes 16777216 | tf_op jit(solution)/shard_map/pallas_call | solution.py:341
  638.2 15.9 %shard_map.88.total = f32[1024,4096]{1,0:T(8,128)} custom-call(s32[2]{0:T(128)} %fusion.1.places, bf16[1024,1024]{1,0:T(8,128)(2,1)} %shard_map.82.rows, bf16[2,768,512]{2,1,0:T(8,128)(2,1)} %collective-permute-done.18.own, bf16[2,768,512]{2,1,0:T(8,128)(2,1)} %copy-done.8, ...), custom_call_target="tpu_custom_call", output_to_operand_aliasing={{}: (6, {})} | custom-call | flops 7516192768 | bytes 16777216 | tf_op jit(solution)/shard_map/pallas_call | solution.py:341
  655.0 15.9 %shard_map.89.total = f32[1024,4096]{1,0:T(8,128)} custom-call(s32[2]{0:T(128)} %fusion.places, bf16[1024,1024]{1,0:T(8,128)(2,1)} %shard_map.81.rows, bf16[2,768,512]{2,1,0:T(8,128)(2,1)} %copy-done, bf16[2,768,512]{2,1,0:T(8,128)(2,1)} %collective-permute-done.13.other, ...), custom_call_target="tpu_custom_call", output_to_operand_aliasing={{}: (6, {})} | custom-call | flops 7516192768 | bytes 16777216 | tf_op jit(solution)/shard_map/pallas_call | solution.py:341
  670.9 23.1 %collective-permute-done.11.own = bf16[2,768,512]{2,1,0:T(8,128)(2,1)} collective-permute-done((bf16[2,768,512]{2,1,0:T(8,128)(2,1)S(1)}, bf16[2,768,512]{2,1,0:T(8,128)(2,1)}, u32[]{:S(2)}, u32[]{:S(2)}) %collective-permute-start.11) | collective-permute-done | bytes 1572896 | tf_op jit(solution)/shard_map/ppermute | solution.py:394
  694.0 16.0 %shard_map.90.total = f32[1024,4096]{1,0:T(8,128)} custom-call(s32[2]{0:T(128)} %fusion.1.places, bf16[1024,1024]{1,0:T(8,128)(2,1)} %shard_map.81.rows, bf16[2,768,512]{2,1,0:T(8,128)(2,1)} %collective-permute-done.11.own, bf16[2,768,512]{2,1,0:T(8,128)(2,1)} %collective-permute-done.12.other, ...), custom_call_target="tpu_custom_call", output_to_operand_aliasing={{}: (6, {})} | custom-call | flops 7516192768 | bytes 16777216 | tf_op jit(solution)/shard_map/pallas_call | solution.py:341
  710.0 11.5 %shard_map.91.total = f32[1024,4096]{1,0:T(8,128)} custom-call(s32[2]{0:T(128)} %fusion.places, bf16[1024,512]{1,0:T(8,128)(2,1)} %shard_map.80.rows, bf16[2,768,256]{2,1,0:T(8,128)(2,1)} %copy-done.2, bf16[2,768,256]{2,1,0:T(8,128)(2,1)} %collective-permute-done.6.other, ...), custom_call_target="tpu_custom_call", output_to_operand_aliasing={{}: (6, {})} | custom-call | flops 3758096384 | bytes 16777216 | tf_op jit(solution)/shard_map/pallas_call | solution.py:341
  721.5 6.1 collective-permute-done.4.own
  728.5 11.5 %shard_map.92 = f32[1024,4096]{1,0:T(8,128)} custom-call(s32[2]{0:T(128)} %fusion.1.places, bf16[1024,512]{1,0:T(8,128)(2,1)} %shard_map.80.rows, bf16[2,768,256]{2,1,0:T(8,128)(2,1)} %copy-done.13, bf16[2,768,256]{2,1,0:T(8,128)(2,1)} %copy-done.12, s32[4,1,1,768]{3,2,1,0:T(1,128)} %get-tuple-element.56.own_cols.own_links, ...), custom_call_target="tpu_custom_call", output_to_operand_aliasing={{}: (6, {})} | custom-call | flops 3758096384 | bytes 16777216 | tf_op jit(solution)/shard_map/pallas_call | solution.py:341
  (127 shorter events, 67.7 us)
Async XLA Ops:
  7.2 48.7 %all-gather.5.cloned.1.call-start = ((), (), s32[]{:S(2)}) async-start(), calls=%async_computation | async-start | bytes 1769472 | tf_op jit(solution)/shard_map/all_gather | solution.py:415
  9.1 110.7 %all-gather.11.cloned.1.call-start = ((), (), s32[]{:S(2)}) async-start(), calls=%async_computation.3 | async-start | bytes 1769472 | tf_op jit(solution)/shard_map/all_gather | solution.py:415
  9.9 173.4 %all-gather.7.cloned.1.call-start = ((), (), s32[]{:S(2)}) async-start(), calls=%async_computation.1 | async-start | bytes 3538944 | tf_op jit(solution)/shard_map/all_gather | solution.py:415
  10.9 233.5 %all-gather.9.cloned.1.call-start = ((), (), s32[]{:S(2)}) async-start(), calls=%async_computation.2 | async-start | bytes 3538944 | tf_op jit(solution)/shard_map/all_gather | solution.py:415
  20.1 517.5 %collective-permute-start.28 = (f32[768,3072]{1,0:T(8,128)}, f32[768,3072]{1,0:T(8,128)}, u32[]{:S(2)}, u32[]{:S(2)}) collective-permute-start(f32[768,3072]{1,0:T(8,128)} %dynamic-slice_bitcast_fusion), channel_id=1, source_target_pairs={{0,8},{8,0},{16,24},{24,16},{1,9},{9,1},{17,25},{25,17},{2,10},{10... | collective-permute-start | bytes 28311560 | tf_op jit(solution)/shard_map/ppermute | solution.py:385
  73.9 48.6 %collective-permute-start.21 = (bf16[768,256]{1,0:T(8,128)(2,1)}, bf16[768,256]{1,0:T(8,128)(2,1)S(1)}, u32[]{:S(2)}, u32[]{:S(2)}) collective-permute-start(bf16[768,256]{1,0:T(8,128)(2,1)} %get-tuple-element.26.own), channel_id=1, source_target_pairs={{0,8},{8,0},{16,24},{24,16},{1,9},{9,1},{17,25},{25,17},{2,10},{10... | collective-permute-start | bytes 1179656 | tf_op jit(solution)/shard_map/ppermute | solution.py:385
  75.7 50.6 %collective-permute-start.22 = (bf16[768,256]{1,0:T(8,128)(2,1)}, bf16[768,256]{1,0:T(8,128)(2,1)S(1)}, u32[]{:S(2)}, u32[]{:S(2)}) collective-permute-start(bf16[768,256]{1,0:T(8,128)(2,1)} %get-tuple-element.26.own), channel_id=1, source_target_pairs={{0,2},{2,4},{4,6},{6,0},{1,3},{3,5},{5,7},{7,1},{8,10},{10,12},{12... | collective-permute-start | bytes 1179656 | tf_op jit(solution)/shard_map/ppermute | solution.py:435
  76.3 50.1 %collective-permute-start.23 = (bf16[768,256]{1,0:T(8,128)(2,1)}, bf16[768,256]{1,0:T(8,128)(2,1)S(1)}, u32[]{:S(2)}, u32[]{:S(2)}) collective-permute-start(bf16[768,256]{1,0:T(8,128)(2,1)} %get-tuple-element.26.own), channel_id=1, source_target_pairs={{0,4},{2,6},{4,0},{6,2},{1,5},{3,7},{5,1},{7,3},{8,12},{10,14},{12... | collective-permute-start | bytes 1179656 | tf_op jit(solution)/shard_map/ppermute | solution.py:435
  77.7 48.7 %collective-permute-start.24 = (bf16[768,256]{1,0:T(8,128)(2,1)}, bf16[768,256]{1,0:T(8,128)(2,1)S(1)}, u32[]{:S(2)}, u32[]{:S(2)}) collective-permute-start(bf16[768,256]{1,0:T(8,128)(2,1)} %get-tuple-element.26.own), channel_id=1, source_target_pairs={{0,6},{2,0},{4,2},{6,4},{1,7},{3,1},{5,3},{7,5},{8,14},{10,8},{12,... | collective-permute-start | bytes 1179656 | tf_op jit(solution)/shard_map/ppermute | solution.py:435
  350.8 32.7 %collective-permute-start.2 = (bf16[768,256]{1,0:T(8,128)(2,1)}, bf16[768,256]{1,0:T(8,128)(2,1)S(1)}, u32[]{:S(2)}, u32[]{:S(2)}) collective-permute-start(bf16[768,256]{1,0:T(8,128)(2,1)} %get-tuple-element.23.own), channel_id=1, source_target_pairs={{0,4},{2,6},{4,0},{6,2},{1,5},{3,7},{5,1},{7,3},{8,12},{10,14},{12... | collective-permute-start | bytes 1179656 | tf_op jit(solution)/shard_map/ppermute | solution.py:435
  352.3 68.5 %collective-permute-start.3 = (bf16[768,256]{1,0:T(8,128)(2,1)}, bf16[768,256]{1,0:T(8,128)(2,1)S(1)}, u32[]{:S(2)}, u32[]{:S(2)}) collective-permute-start(bf16[768,256]{1,0:T(8,128)(2,1)} %get-tuple-element.23.own), channel_id=1, source_target_pairs={{0,6},{2,0},{4,2},{6,4},{1,7},{3,1},{5,3},{7,5},{8,14},{10,8},{12,... | collective-permute-start | bytes 1179656 | tf_op jit(solution)/shard_map/ppermute | solution.py:435
  353.1 81.0 %collective-permute-start.8 = (bf16[768,512]{1,0:T(8,128)(2,1)}, bf16[768,512]{1,0:T(8,128)(2,1)S(1)}, u32[]{:S(2)}, u32[]{:S(2)}) collective-permute-start(bf16[768,512]{1,0:T(8,128)(2,1)} %get-tuple-element.24.own), channel_id=1, source_target_pairs={{0,2},{2,4},{4,6},{6,0},{1,3},{3,5},{5,7},{7,1},{8,10},{10,12},{12... | collective-permute-start | bytes 2359304 | tf_op jit(solution)/shard_map/ppermute | solution.py:435
  358.4 109.4 %collective-permute-start.9 = (bf16[768,512]{1,0:T(8,128)(2,1)}, bf16[768,512]{1,0:T(8,128)(2,1)S(1)}, u32[]{:S(2)}, u32[]{:S(2)}) collective-permute-start(bf16[768,512]{1,0:T(8,128)(2,1)} %get-tuple-element.24.own), channel_id=1, source_target_pairs={{0,4},{2,6},{4,0},{6,2},{1,5},{3,7},{5,1},{7,3},{8,12},{10,14},{12... | collective-permute-start | bytes 2359304 | tf_op jit(solution)/shard_map/ppermute | solution.py:435
  383.5 37.5 %collective-permute-start = (bf16[768,256]{1,0:T(8,128)(2,1)S(1)}, bf16[768,256]{1,0:T(8,128)(2,1)S(1)}, u32[]{:S(2)}, u32[]{:S(2)}) collective-permute-start(bf16[768,256]{1,0:T(8,128)(2,1)S(1)} %copy-done.15), channel_id=1, source_target_pairs={{0,8},{8,0},{16,24},{24,16},{1,9},{9,1},{17,25},{25,17},{2,10},{10... | collective-permute-start | bytes 1179656 | tf_op jit(solution)/shard_map/ppermute | solution.py:385
  420.8 67.6 %collective-permute-start.10 = (bf16[768,512]{1,0:T(8,128)(2,1)}, bf16[768,512]{1,0:T(8,128)(2,1)}, u32[]{:S(2)}, u32[]{:S(2)}) collective-permute-start(bf16[768,512]{1,0:T(8,128)(2,1)} %get-tuple-element.24.own), channel_id=1, source_target_pairs={{0,6},{2,0},{4,2},{6,4},{1,7},{3,1},{5,3},{7,5},{8,14},{10,8},{12,... | collective-permute-start | bytes 2359304 | tf_op jit(solution)/shard_map/ppermute | solution.py:435
  421.0 80.5 %collective-permute-start.15 = (bf16[768,512]{1,0:T(8,128)(2,1)}, bf16[768,512]{1,0:T(8,128)(2,1)}, u32[]{:S(2)}, u32[]{:S(2)}) collective-permute-start(bf16[768,512]{1,0:T(8,128)(2,1)} %get-tuple-element.25.own), channel_id=1, source_target_pairs={{0,2},{2,4},{4,6},{6,0},{1,3},{3,5},{5,7},{7,1},{8,10},{10,12},{12... | collective-permute-start | bytes 2359304 | tf_op jit(solution)/shard_map/ppermute | solution.py:435
  434.1 84.3 %collective-permute-start.16 = (bf16[768,512]{1,0:T(8,128)(2,1)}, bf16[768,512]{1,0:T(8,128)(2,1)S(1)}, u32[]{:S(2)}, u32[]{:S(2)}) collective-permute-start(bf16[768,512]{1,0:T(8,128)(2,1)} %get-tuple-element.25.own), channel_id=1, source_target_pairs={{0,4},{2,6},{4,0},{6,2},{1,5},{3,7},{5,1},{7,3},{8,12},{10,14},{12... | collective-permute-start | bytes 2359304 | tf_op jit(solution)/shard_map/ppermute | solution.py:435
  467.8 54.2 %collective-permute-start.17 = (bf16[768,512]{1,0:T(8,128)(2,1)}, bf16[768,512]{1,0:T(8,128)(2,1)S(1)}, u32[]{:S(2)}, u32[]{:S(2)}) collective-permute-start(bf16[768,512]{1,0:T(8,128)(2,1)} %get-tuple-element.25.own), channel_id=1, source_target_pairs={{0,6},{2,0},{4,2},{6,4},{1,7},{3,1},{5,3},{7,5},{8,14},{10,8},{12,... | collective-permute-start | bytes 2359304 | tf_op jit(solution)/shard_map/ppermute | solution.py:435
  488.4 36.4 %collective-permute-start.14 = (bf16[768,512]{1,0:T(8,128)(2,1)}, bf16[768,512]{1,0:T(8,128)(2,1)}, u32[]{:S(2)}, u32[]{:S(2)}) collective-permute-start(bf16[768,512]{1,0:T(8,128)(2,1)} %get-tuple-element.25.own), channel_id=1, source_target_pairs={{0,8},{8,0},{16,24},{24,16},{1,9},{9,1},{17,25},{25,17},{2,10},{10... | collective-permute-start | bytes 2359304 | tf_op jit(solution)/shard_map/ppermute | solution.py:385
  501.5 30.3 %collective-permute-start.7 = (bf16[768,512]{1,0:T(8,128)(2,1)}, bf16[768,512]{1,0:T(8,128)(2,1)}, u32[]{:S(2)}, u32[]{:S(2)}) collective-permute-start(bf16[768,512]{1,0:T(8,128)(2,1)} %get-tuple-element.24.own), channel_id=1, source_target_pairs={{0,8},{8,0},{16,24},{24,16},{1,9},{9,1},{17,25},{25,17},{2,10},{10... | collective-permute-start | bytes 2359304 | tf_op jit(solution)/shard_map/ppermute | solution.py:385
  518.4 18.6 %collective-permute-start.27 = (bf16[2,768,256]{2,1,0:T(8,128)(2,1)}, bf16[2,768,256]{2,1,0:T(8,128)(2,1)}, u32[]{:S(2)}, u32[]{:S(2)}) collective-permute-start(bf16[2,768,256]{2,1,0:T(8,128)(2,1)} %pad_maximum_fusion.11), channel_id=1, source_target_pairs={{0,8},{1,9},{2,10},{3,11},{4,12},{5,13},{6,14},{7,15},{8,0},{9,1},... | collective-permute-start | bytes 2359304 | tf_op jit(solution)/shard_map/ppermute | solution.py:394
  522.0 85.7 %collective-permute-start.26 = (bf16[2,768,256]{2,1,0:T(8,128)(2,1)}, bf16[2,768,256]{2,1,0:T(8,128)(2,1)}, u32[]{:S(2)}, u32[]{:S(2)}) collective-permute-start(bf16[2,768,256]{2,1,0:T(8,128)(2,1)} %pad_maximum_fusion.11), channel_id=1, source_target_pairs={{0,9},{1,8},{2,11},{3,10},{4,13},{5,12},{6,15},{7,14},{8,1},{9,0},... | collective-permute-start | bytes 2359304 | tf_op jit(solution)/shard_map/ppermute | solution.py:394
  524.8 82.5 %collective-permute-start.25 = (bf16[2,768,256]{2,1,0:T(8,128)(2,1)S(1)}, bf16[2,768,256]{2,1,0:T(8,128)(2,1)}, u32[]{:S(2)}, u32[]{:S(2)}) collective-permute-start(bf16[2,768,256]{2,1,0:T(8,128)(2,1)S(1)} %pad_maximum_fusion.10.own), channel_id=1, source_target_pairs={{0,1},{1,0},{2,3},{3,2},{4,5},{5,4},{6,7},{7,6},{8,9},{9,8},{10,11... | collective-permute-start | bytes 2359304 | tf_op jit(solution)/shard_map/ppermute | solution.py:394
  531.9 88.0 %collective-permute-start.20 = (bf16[2,768,512]{2,1,0:T(8,128)(2,1)}, bf16[2,768,512]{2,1,0:T(8,128)(2,1)}, u32[]{:S(2)}, u32[]{:S(2)}) collective-permute-start(bf16[2,768,512]{2,1,0:T(8,128)(2,1)} %pad_maximum_fusion.6), channel_id=1, source_target_pairs={{0,8},{1,9},{2,10},{3,11},{4,12},{5,13},{6,14},{7,15},{8,0},{9,1},... | collective-permute-start | bytes 4718600 | tf_op jit(solution)/shard_map/ppermute | solution.py:394
  537.0 99.7 %collective-permute-start.19 = (bf16[2,768,512]{2,1,0:T(8,128)(2,1)}, bf16[2,768,512]{2,1,0:T(8,128)(2,1)S(1)}, u32[]{:S(2)}, u32[]{:S(2)}) collective-permute-start(bf16[2,768,512]{2,1,0:T(8,128)(2,1)} %pad_maximum_fusion.6), channel_id=1, source_target_pairs={{0,9},{1,8},{2,11},{3,10},{4,13},{5,12},{6,15},{7,14},{8,1},{9,0},... | collective-permute-start | bytes 4718600 | tf_op jit(solution)/shard_map/ppermute | solution.py:394
  537.8 99.7 %collective-permute-start.18 = (bf16[2,768,512]{2,1,0:T(8,128)(2,1)S(1)}, bf16[2,768,512]{2,1,0:T(8,128)(2,1)}, u32[]{:S(2)}, u32[]{:S(2)}) collective-permute-start(bf16[2,768,512]{2,1,0:T(8,128)(2,1)S(1)} %pad_maximum_fusion.5.own), channel_id=1, source_target_pairs={{0,1},{1,0},{2,3},{3,2},{4,5},{5,4},{6,7},{7,6},{8,9},{9,8},{10,11... | collective-permute-start | bytes 4718600 | tf_op jit(solution)/shard_map/ppermute | solution.py:394
  607.3 46.9 %collective-permute-start.13 = (bf16[2,768,512]{2,1,0:T(8,128)(2,1)S(1)}, bf16[2,768,512]{2,1,0:T(8,128)(2,1)}, u32[]{:S(2)}, u32[]{:S(2)}) collective-permute-start(bf16[2,768,512]{2,1,0:T(8,128)(2,1)S(1)} %pad_maximum_fusion.4), channel_id=1, source_target_pairs={{0,8},{1,9},{2,10},{3,11},{4,12},{5,13},{6,14},{7,15},{8,0},{9,1},... | collective-permute-start | bytes 4718600 | tf_op jit(solution)/shard_map/ppermute | solution.py:394
  607.7 63.2 %collective-permute-start.12 = (bf16[2,768,512]{2,1,0:T(8,128)(2,1)S(1)}, bf16[2,768,512]{2,1,0:T(8,128)(2,1)}, u32[]{:S(2)}, u32[]{:S(2)}) collective-permute-start(bf16[2,768,512]{2,1,0:T(8,128)(2,1)S(1)} %pad_maximum_fusion.4), channel_id=1, source_target_pairs={{0,9},{1,8},{2,11},{3,10},{4,13},{5,12},{6,15},{7,14},{8,1},{9,0},... | collective-permute-start | bytes 4718600 | tf_op jit(solution)/shard_map/ppermute | solution.py:394
  619.9 74.1 %collective-permute-start.11 = (bf16[2,768,512]{2,1,0:T(8,128)(2,1)S(1)}, bf16[2,768,512]{2,1,0:T(8,128)(2,1)}, u32[]{:S(2)}, u32[]{:S(2)}) collective-permute-start(bf16[2,768,512]{2,1,0:T(8,128)(2,1)S(1)} %pad_maximum_fusion.3.own), channel_id=1, source_target_pairs={{0,1},{1,0},{2,3},{3,2},{4,5},{5,4},{6,7},{7,6},{8,9},{9,8},{10,11... | collective-permute-start | bytes 4718600 | tf_op jit(solution)/shard_map/ppermute | solution.py:394
  636.7 73.3 %collective-permute-start.6 = (bf16[2,768,256]{2,1,0:T(8,128)(2,1)S(1)}, bf16[2,768,256]{2,1,0:T(8,128)(2,1)}, u32[]{:S(2)}, u32[]{:S(2)}) collective-permute-start(bf16[2,768,256]{2,1,0:T(8,128)(2,1)S(1)} %copy-done.11), channel_id=1, source_target_pairs={{0,8},{1,9},{2,10},{3,11},{4,12},{5,13},{6,14},{7,15},{8,0},{9,1},... | collective-permute-start | bytes 2359304 | tf_op jit(solution)/shard_map/ppermute | solution.py:394
  637.5 84.0 %collective-permute-start.5 = (bf16[2,768,256]{2,1,0:T(8,128)(2,1)S(1)}, bf16[2,768,256]{2,1,0:T(8,128)(2,1)S(1)}, u32[]{:S(2)}, u32[]{:S(2)}) collective-permute-start(bf16[2,768,256]{2,1,0:T(8,128)(2,1)S(1)} %copy-done.11), channel_id=1, source_target_pairs={{0,9},{1,8},{2,11},{3,10},{4,13},{5,12},{6,15},{7,14},{8,1},{9,0},... | collective-permute-start | bytes 2359304 | tf_op jit(solution)/shard_map/ppermute | solution.py:394
  654.1 73.5 %collective-permute-start.4 = (bf16[2,768,256]{2,1,0:T(8,128)(2,1)S(1)}, bf16[2,768,256]{2,1,0:T(8,128)(2,1)S(1)}, u32[]{:S(2)}, u32[]{:S(2)}) collective-permute-start(bf16[2,768,256]{2,1,0:T(8,128)(2,1)S(1)} %pad_maximum_fusion.8.own), channel_id=1, source_target_pairs={{0,1},{1,0},{2,3},{3,2},{4,5},{5,4},{6,7},{7,6},{8,9},{9,8},{10,11... | collective-permute-start | bytes 2359304 | tf_op jit(solution)/shard_map/ppermute | solution.py:394
  (20 other events, 476.9 us)
Sparse Core Ops, SparseCore 0:
  10.8 45.0 all-gather.4
  58.1 61.7 all-gather.10
  122.0 61.1 all-gather.6
  185.3 59.0 all-gather.8

commit v2 on v1

v2 whole, which is shorter than its diff:
```python
import math

import jax
import jax.numpy as jnp
from jax import lax
from jax.experimental import pallas as pl
from jax.experimental.pallas import tpu as pltpu
from jax.sharding import PartitionSpec as P

ROWS = ("prow", "pcol")
bf16 = jnp.bfloat16
f32 = jnp.float32
LANES = 128
SUBS = 8
GROUP = 32
VMEM_LIMIT = 56 << 20


def panel_widths(order):
    narrow = order // 6
    return (narrow, 2 * narrow, 2 * narrow, narrow)


def split(x):
    top = x.astype(bf16)
    return top, (x - top.astype(f32)).astype(bf16)


def left_parts(x):
    top, low = split(x)
    return jnp.concatenate([top, top, low], axis=1)


def right_parts(x):
    top, low = split(x)
    return jnp.concatenate([top, low, top], axis=1)


def nt(a, b):
    return lax.dot_general(a, b, (((1,), (1,)), ((), ())), preferred_element_type=f32)


def nn(a, b):
    return jnp.dot(a, b, preferred_element_type=f32)


def spread_lane(x, lane):
    return jnp.broadcast_to(x[:, lane:lane + 1], (SUBS, LANES))


def spread_sub(x, sub):
    return jnp.broadcast_to(x[sub:sub + 1, :], (SUBS, LANES))


def factor_square(square):
    lane = lax.broadcasted_iota(jnp.int32, (SUBS, LANES), 1)
    sub = lax.broadcasted_iota(jnp.int32, (SUBS, LANES), 0)
    count = LANES // SUBS
    span = GROUP // SUBS
    state = [square[SUBS * r:SUBS * (r + 1), :] for r in range(count)]
    inverses = []
    for b in range(count):
        first = SUBS * b
        last = (b // span + 1) * span
        block = state[b]
        inside = (lane >= first) & (lane < first + SUBS)
        columns = [spread_lane(block, first + k) for k in range(SUBS)]
        d = [
            [spread_sub(columns[k], i) if k >= i else None for k in range(SUBS)]
            for i in range(SUBS)
        ]
        packed = jnp.where(inside, (lane - first == sub).astype(f32), block)
        rows = [spread_sub(packed, i) for i in range(SUBS)]
        follow = b + 1 < last
        if follow:
            ahead = state[b + 1]
            beside = [spread_lane(ahead, first + k) for k in range(SUBS)]
            ahead = jnp.where(inside, 0.0, ahead)
        scales, steps = [], []
        for i in range(SUBS):
            scale = lax.rsqrt(d[i][i])
            scales.append(scale)
            step = [d[i][k] * scale if k > i else None for k in range(SUBS)]
            steps.append(step)
            rows[i] = rows[i] * scale
            if follow:
                beside[i] = beside[i] * scale
                ahead = ahead - beside[i] * rows[i]
            for k in range(i + 1, SUBS):
                for m in range(k, SUBS):
                    d[k][m] = d[k][m] - step[k] * step[m]
                rows[k] = rows[k] - step[k] * rows[i]
                if follow:
                    beside[k] = beside[k] - step[k] * beside[i]
        whole = rows[0]
        for i in range(1, SUBS):
            whole = jnp.where(sub == i, rows[i], whole)
        inverses.append(whole)
        if follow:
            state[b + 1] = ahead
        if b + 2 < last:
            back = [None] * SUBS
            for i in reversed(range(SUBS)):
                total = rows[i]
                for k in range(i + 1, SUBS):
                    total = total - steps[i][k] * back[k]
                back[i] = total * scales[i]
            for r in range(b + 2, last):
                below = state[r]
                left = [spread_lane(below, first + k) for k in range(SUBS)]
                below = jnp.where(inside, 0.0, below)
                for k in range(SUBS):
                    below = below - left[k] * back[k]
                state[r] = below
        if b + 1 == last and last < count:
            start = GROUP * (b // span)
            solved = jnp.concatenate(
                [
                    jnp.where((lane >= SUBS * (g + 1)) & (lane < SUBS * last), 0.0, inverses[g])
                    for g in range(b + 1 - span, b + 1)
                ],
                axis=0,
            )
            after = jnp.concatenate(state[last:], axis=0)
            own = slice(start, start + GROUP)
            left = nt(left_parts(after[:, own]), right_parts(solved[:, own]))
            top, low = split(solved)
            change = nn(left_parts(left), jnp.concatenate([top, low, top], axis=0))
            for r in range(last, count):
                at = SUBS * (r - last)
                done = (lane >= start) & (lane < start + GROUP)
                state[r] = jnp.where(done, 0.0, state[r]) - change[at:at + SUBS, :]
    return jnp.concatenate(
        [jnp.where(lane < SUBS * (b + 1), inverses[b], 0.0) for b in range(count)], axis=0
    )


def largest_tile(rows):
    return next(t for t in (256, 128, 64, 32, 16, 8) if rows % t == 0)


def panel_kernel(first, base, bases, pcols, *refs):
    refs = list(refs)
    across, shares, refs = refs[0], refs[1:1 + pcols], refs[1 + pcols:]
    before = len(bases)
    earlier = [(refs[2 * q], refs[2 * q + 1]) for q in range(before)]
    refs = refs[2 * before:]
    lower_in, _, pivot, lower, rounded, tops = refs[:6]
    crowns = refs[6:]
    width = pivot.shape[1]
    count = width // LANES
    skip = first - base
    bottom = skip + width
    for q in range(before):
        for t in range(count):
            at = first - bases[q] + t * LANES
            crowns[q][t * LANES:(t + 1) * LANES, :] = right_parts(
                earlier[q][0][at:at + LANES, :]
            )
    share_rows = shares[0].shape[1]
    for apart in range(pcols):
        source = lax.rem(across[0] - apart + pcols, pcols)
        for r in range(shares[apart].shape[0]):
            at = pl.multiple_of((r * pcols + source) * share_rows, 8)
            pivot[pl.ds(at, share_rows), :] = shares[apart][r]
    pltpu.sync_copy(lower_in.at[:, first:first + width], lower)

    def subtract(target, pasts, offsets):
        tile = largest_tile(target.shape[0])

        @pl.loop(0, target.shape[0] // tile)
        def _(t):
            at = pl.multiple_of(t * tile, tile)
            values = target[pl.ds(at, tile), :]
            for q in range(before):
                past = pasts[q][pl.ds(pl.multiple_of(offsets[q] + at, 8), tile), :]
                values = values - nt(left_parts(past), crowns[q][...])
            target[pl.ds(at, tile), :] = values

    if before:
        subtract(pivot, [past for past, _ in earlier], [base - b for b in bases])
        subtract(lower, [past for _, past in earlier], [0] * before)
    if skip:
        pivot[0:skip, :] = jnp.zeros((skip, width), f32)

    @pl.loop(0, count)
    def _(k):
        here = pl.ds(pl.multiple_of(k * LANES, LANES), LANES)
        corner = pl.ds(pl.multiple_of(skip + k * LANES, LANES), LANES)
        square = pivot[corner, here]
        solver = right_parts(factor_square(square))
        below = lax.broadcasted_iota(jnp.int32, (LANES, LANES), 0) >= lax.broadcasted_iota(
            jnp.int32, (LANES, LANES), 1
        )
        pivot[corner, here] = jnp.where(below, nt(left_parts(square), solver), 0.0)
        for t in range(count):
            block = slice(skip + t * LANES, skip + (t + 1) * LANES)

            @pl.when(t < k)
            def _():
                pivot[block, here] = jnp.zeros((LANES, LANES), f32)

            @pl.when(t > k)
            def _():
                solved = nt(left_parts(pivot[block, here]), solver)
                pivot[block, here] = solved
                tops[t * LANES:(t + 1) * LANES, :] = right_parts(solved)

        for c in range(1, count):
            cols = slice(c * LANES, (c + 1) * LANES)

            @pl.when(c > k)
            def _():
                block = slice(skip + c * LANES, bottom)
                solved = left_parts(pivot[block, here])
                pivot[block, cols] -= nt(solved, tops[cols, :])

        def run(ref, start, rows):
            tile = largest_tile(rows)

            @pl.loop(0, rows // tile)
            def _(t):
                band = pl.ds(pl.multiple_of(start + t * tile, 8), tile)
                solved = nt(left_parts(ref[band, here]), solver)
                ref[band, here] = solved
                parts = left_parts(solved)
                for c in range(1, count):
                    cols = slice(c * LANES, (c + 1) * LANES)

                    @pl.when(c > k)
                    def _():
                        ref[band, cols] -= nt(parts, tops[cols, :])

        if pivot.shape[0] > bottom:
            run(pivot, bottom, pivot.shape[0] - bottom)
        run(lower, 0, lower.shape[0])

    tile = largest_tile(lower.shape[0])

    @pl.loop(0, lower.shape[0] // tile)
    def _(t):
        here = pl.ds(pl.multiple_of(t * tile, tile), tile)
        rounded[here, :] = lower[here, :].astype(bf16)


def factor_panel(first, across, shares, lower, earlier, after):
    prows, share_rows, width = shares[0].shape
    rows = len(shares) * prows * share_rows
    order = lower.shape[1]
    base = order - rows
    flat = [past for pair in earlier for past in pair]
    in_vmem = pl.BlockSpec(memory_space=pltpu.VMEM)
    anywhere = pl.BlockSpec(memory_space=pl.ANY)
    bases = [order - past.shape[0] for past, _ in earlier]
    return pl.pallas_call(
        lambda *refs: panel_kernel(first, base, bases, len(shares), *refs),
        out_shape=(
            jax.ShapeDtypeStruct((rows, width), f32),
            jax.ShapeDtypeStruct((lower.shape[0], width), f32),
            jax.ShapeDtypeStruct((lower.shape[0], width), bf16),
        ),
        in_specs=[pl.BlockSpec(memory_space=pltpu.SMEM)]
        + [in_vmem] * (len(shares) + len(flat))
        + [anywhere] * 2,
        out_specs=[in_vmem] * 3,
        scratch_shapes=[pltpu.VMEM((width, 3 * LANES), bf16)]
        + [pltpu.VMEM((width, 3 * past.shape[1]), bf16) for past, _ in earlier],
        compiler_params=pltpu.CompilerParams(vmem_limit_bytes=VMEM_LIMIT),
        cost_estimate=pl.CostEstimate(
            flops=width * 50000000,
            bytes_accessed=10 * width * (rows + lower.shape[0]),
            transcendentals=0,
        ),
    )(across, *shares, *flat, lower, after)


def one_hot(links, window):
    places = lax.broadcasted_iota(jnp.int32, (window, links.shape[1]), 0)
    return (places == links).astype(bf16)


def rest_kernel(first, values, row_links, col_links, parent, out, table, placed):
    window = out.shape[0]
    rows = values.shape[0]

    @pl.when(pl.program_id(0) == 0)
    def _():
        spread = one_hot(row_links[0], window)
        table[:, :rows] = spread
        table[:, rows:] = spread

    top, low = split(values[...])
    for i in range(col_links.shape[0]):
        spread = one_hot(col_links[i, 0], window)
        block, area = slice(i * rows, (i + 1) * rows), slice(i * window, (i + 1) * window)
        placed[:rows, area] = nt(top[:, block], spread).astype(bf16)
        placed[rows:, area] = nt(low[:, block], spread).astype(bf16)
    tile = largest_tile(window)

    @pl.loop(0, window // tile)
    def _(t):
        here = pl.ds(pl.multiple_of(t * tile, tile), tile)
        out[here, :] = parent[here, :] + nn(table[here, :], placed[...])


def add_rest(parent, values, half, row_links, col_links, in_place):
    window = parent.shape[0]
    rows = values.shape[0]
    group = LANES // math.gcd(LANES, rows)
    steps = parent.shape[1] // window // group
    area = pl.BlockSpec((window, group * window), lambda w, half: (0, w))
    return pl.pallas_call(
        rest_kernel,
        out_shape=jax.ShapeDtypeStruct(parent.shape, f32),
        grid_spec=pltpu.PrefetchScalarGridSpec(
            num_scalar_prefetch=1,
            grid=(steps,),
            in_specs=[
                pl.BlockSpec((rows, group * rows), lambda w, half: (0, half[0] * steps + w)),
                pl.BlockSpec((1, 1, rows), lambda w, half: (0, 0, 0)),
                pl.BlockSpec((group, 1, 1, rows), lambda w, half: (w, 0, 0, 0)),
                area,
            ],
            out_specs=area,
            scratch_shapes=[
                pltpu.VMEM((window, 2 * rows), bf16),
                pltpu.VMEM((2 * rows, group * window), bf16),
            ],
        ),
        input_output_aliases={4: 0} if in_place else {},
        compiler_params=pltpu.CompilerParams(vmem_limit_bytes=VMEM_LIMIT),
        cost_estimate=pl.CostEstimate(
            flops=4 * rows * parent.size + 4 * rows * rows * parent.shape[1],
            bytes_accessed=8 * parent.size + 4 * rows * rows * steps * group,
            transcendentals=0,
        ),
    )(half, values, row_links, col_links, parent)


def rows_kernel(own, other, own_links, other_links, out):
    window, width = out.shape[0], own.shape[1]
    for source, (values, links) in enumerate(((own, own_links), (other, other_links))):
        out[:, source * width:(source + 1) * width] = nn(
            one_hot(links[0], window), values[...]
        ).astype(bf16)


def spread_rows(own, other, row_links, window):
    return pl.pallas_call(
        rows_kernel,
        out_shape=jax.ShapeDtypeStruct((window, 2 * own.shape[1]), bf16),
        compiler_params=pltpu.CompilerParams(vmem_limit_bytes=VMEM_LIMIT),
        cost_estimate=pl.CostEstimate(
            flops=4 * window * own.size, bytes_accessed=12 * own.size, transcendentals=0
        ),
    )(own, other, *row_links)


def update_kernel(places, rows, own, other, own_links, other_links, total, out, cols):
    window, width = cols.shape[0], own.shape[2]

    @pl.when(pl.program_id(1) == 0)
    def _():
        for source, (values, links) in enumerate(((own, own_links), (other, other_links))):
            cols[:, source * width:(source + 1) * width] = nn(
                one_hot(links[0, 0], window), values[0]
            ).astype(bf16)

    out[...] = total[...] - nt(rows[...], cols[...])


def update_windows(total, rows, own, other, places, col_links):
    window = total.shape[0]
    count, children, width = own.shape
    tile = largest_tile(window)
    block = pl.BlockSpec((1, children, width), lambda i, t, places: (i, 0, 0))
    link = pl.BlockSpec((1, 1, 1, children), lambda i, t, places: (places[i], 0, 0, 0))
    area = pl.BlockSpec((tile, window), lambda i, t, places: (t, places[i]))
    return pl.pallas_call(
        update_kernel,
        out_shape=jax.ShapeDtypeStruct(total.shape, f32),
        grid_spec=pltpu.PrefetchScalarGridSpec(
            num_scalar_prefetch=1,
            grid=(count, window // tile),
            in_specs=[
                pl.BlockSpec((tile, 2 * width), lambda i, t, places: (t, 0)),
                block,
                block,
                link,
                link,
                area,
            ],
            out_specs=area,
            scratch_shapes=[pltpu.VMEM((window, 2 * width), bf16)],
        ),
        input_output_aliases={6: 0},
        compiler_params=pltpu.CompilerParams(vmem_limit_bytes=VMEM_LIMIT),
        cost_estimate=pl.CostEstimate(
            flops=4 * count * window * width * (window + children),
            bytes_accessed=8 * count * window * window,
            transcendentals=0,
        ),
    )(places, rows, own, other, *col_links, total)


def local(front_pivot, front_lower, front_rest, parent_front, relation):
    leaves, prows, pcols = (lax.axis_size(a) for a in ("leaf", "prow", "pcol"))
    position = lax.axis_index(ROWS)
    across = lax.axis_index("pcol")
    pivot_rows, lower_rows = front_pivot[0], front_lower[0]
    rest_rows, parent_rows = front_rest[0], parent_front[0]
    rows_here, pivot_order = pivot_rows.shape
    block_rows, child_order = rest_rows.shape
    window = parent_rows.shape[0]
    child_half = child_order // 2
    blocks = child_half // block_rows
    near = prows // 2
    leaf_index = lax.axis_index("leaf")
    side = leaf_index % 2
    partner = leaf_index + 1 - 2 * side

    def to_sibling(value):
        return lax.ppermute(value, "leaf", [(g, g ^ 1) for g in range(leaves)])

    def to_cols(value, apart, swap):
        pairs = [
            ((g * prows + r) * pcols + c, ((g ^ swap) * prows + r) * pcols + (c + apart) % pcols)
            for g in range(leaves)
            for r in range(prows)
            for c in range(pcols)
        ]
        return lax.ppermute(value, ("leaf",) + ROWS, pairs)

    def links_of(child):
        links = lax.dynamic_index_in_dim(relation, child, 0, keepdims=False)
        rows = lax.dynamic_slice_in_dim(links, position * block_rows, block_rows, 0)
        cols = lax.dynamic_slice_in_dim(links, side * child_half, child_half, 0)
        cols = cols.reshape(blocks, 1, 1, block_rows)
        first = side * blocks + jnp.arange(blocks, dtype=jnp.int32)
        return (
            (rows - position * window).reshape(1, 1, block_rows),
            cols - first.reshape(blocks, 1, 1, 1) * window,
        )

    own_row_links, own_col_links = links_of(leaf_index)
    other_row_links, other_col_links = links_of(partner)
    row_links = (own_row_links, other_row_links)
    col_links = (own_col_links, other_col_links)

    widths = panel_widths(pivot_order)
    starts = [sum(widths[:p]) for p in range(len(widths))]
    column_blocks = []
    for s, w in zip(starts, widths):
        mine = lax.all_gather(pivot_rows[:, s:s + w], "prow", axis=0)[s // (rows_here * pcols):]
        column_blocks.append([mine] + [to_cols(mine, apart, 0) for apart in range(1, pcols)])

    leaving = lax.dynamic_slice_in_dim(rest_rows, (1 - side) * child_half, child_half, 1)
    arrived = to_sibling(leaving)
    half = side.astype(jnp.int32).reshape(1)
    start_total = add_rest(parent_rows, rest_rows, half, own_row_links, own_col_links, False)
    total = add_rest(
        start_total, arrived, jnp.zeros((1,), jnp.int32), other_row_links, other_col_links, True
    )

    done, panels = [], []
    across_one = across.astype(jnp.int32).reshape(1)
    for p, (s, shares) in enumerate(zip(starts, column_blocks)):
        wait_for = (start_total, total)[p] if p < 2 else done[-1][0]
        pivot, lower, rounded = factor_panel(s, across_one, shares, lower_rows, done, wait_for)
        done.append((pivot, lower))
        other = to_sibling(rounded)
        line = lax.all_gather(rounded, "prow", axis=0)
        kept = lax.dynamic_slice_in_dim(line, side * near, near, 0)
        sent = lax.dynamic_slice_in_dim(line, (1 - side) * near, near, 0)
        panels.append((rounded, other, kept, sent))

    for rounded, other, kept, sent in panels:
        rows = spread_rows(rounded, other, row_links, window)
        for apart in range(pcols):
            own = to_cols(kept, apart, 0) if apart else kept
            sibling = to_cols(sent, apart, 1)
            places = jnp.arange(near, dtype=jnp.int32) * pcols + lax.rem(
                across - apart + pcols, pcols
            ).astype(jnp.int32)
            total = update_windows(total, rows, own, sibling, places, col_links)

    factor_rows = jnp.concatenate(
        [
            lax.dynamic_slice_in_dim(
                jnp.concatenate([jnp.zeros((pivot_order - pivot.shape[0], w), f32), pivot], axis=0),
                position * rows_here,
                rows_here,
                0,
            )
            for s, w, (pivot, _) in zip(starts, widths, done)
        ],
        axis=1,
    )
    lower_out = jnp.concatenate([lower for _, lower in done], axis=1)
    return (factor_rows[None], lower_out[None], total[None])


def solution(mesh):
    whole = P("leaf", ROWS, None)
    return jax.shard_map(
        local,
        mesh=mesh,
        in_specs=(whole, whole, whole, whole, P()),
        out_specs=(whole, whole, whole),
        check_vma=False,
    )
```

time: 753 us -> 541 us (0.72)
  waiting for transfers between devices: 351 us -> 77.4 us
  blocking collectives: 0 us -> 40.8 us
  Pallas kernels: 302 us -> 333 us
  starting transfers between devices: 33 us -> 22.3 us
  other arithmetic: 15.8 us -> 7.02 us
    all_gather x4 -> x6, waiting for transfers between devices: 181 us -> 0.04 us  [the longest x2 0.04 us: local(): lax.all_gather(pivot_rows[:, s:s + w], 'prow', axis=0)]
    ppermute x12 -> x0, waiting for transfers between devices: 139 us -> none  [local(): lax.ppermute(rounded, 'prow', [(r, (r + step) % prows) for r in range(pro...]
    ppermute x12 -> x16, waiting for transfers between devices: 29.3 us -> 77.2 us  [to_cols(): return lax.ppermute(value, ('leaf',) + ROWS, pairs)]
    all_gather x0 -> x2, blocking collectives: none -> 40.8 us  [local(): lax.all_gather(pivot_rows[:, s:s + w], 'prow', axis=0)]
    pallas_call x8, Pallas kernels: 110 us -> 126 us  [update_windows(): pl.pallas_call(update_kernel, out_shape=jax.ShapeDtypeStruct(total.shape,...]
    slice x5 -> x2, local copies, waits for them, and re-layouts: 14.4 us -> 1.2 us  [local(): lax.all_gather(pivot_rows[:, s:s + w], 'prow', axis=0)]
    dynamic_slice x6 -> x8, local copies, waits for them, and re-layouts: 1.69 us -> 12.9 us  [the longest x4 10.6 us: local(): sent = lax.dynamic_slice_in_dim(line, (1 - side) * near, near, 0)]
    ppermute x12 -> x0, starting transfers between devices: 11.2 us -> none  [local(): lax.ppermute(rounded, 'prow', [(r, (r + step) % prows) for r in range(pro...]
  transfers between devices with their start and end apart: 33 -> 27, of which waited for: 15 -> 4; matrix products, arithmetic and copies ran while one was open for 6% -> 4% of each run, Pallas kernels for 39% -> 60%
where the time goes in v2:
time: 541 us; the launch traced here: 530 us
  Pallas kernels  333 us (62%)
  waiting for transfers between devices  77.4 us (14%)
  blocking collectives  40.8 us (8%)
  local copies, waits for them, and re-layouts  34.6 us (6%)
  starting transfers between devices  22.3 us (4%)
  between operations  14.6 us (3%)
  other arithmetic  7.02 us (1%)
    pallas_call x4, Pallas kernels, factor_panel(): pl.pallas_call(lambda *refs: panel_kernel(first, base, bases, len(shares)...  128 us
    pallas_call x8, Pallas kernels, update_windows(): pl.pallas_call(update_kernel, out_shape=jax.ShapeDtypeStruct(total.shape,...  126 us
    ppermute x16, waiting for transfers between devices, to_cols(): return lax.ppermute(value, ('leaf',) + ROWS, pairs)  77.2 us
    pallas_call x2, Pallas kernels, add_rest(): pl.pallas_call(rest_kernel, out_shape=jax.ShapeDtypeStruct(parent.shape,...  63.7 us
    all_gather x2, blocking collectives, local(): lax.all_gather(pivot_rows[:, s:s + w], 'prow', axis=0)  40.8 us
    pallas_call x4, Pallas kernels, spread_rows(): pl.pallas_call(rows_kernel, out_shape=jax.ShapeDtypeStruct((window, 2 * o...  15.1 us
    ppermute x16, starting transfers between devices, to_cols(): return lax.ppermute(value, ('leaf',) + ROWS, pairs)  12 us
  transfers between devices with their start and end apart: 27, of which 4 were waited for; matrix products, arithmetic and copies ran while one was open for 4% of the time, Pallas kernels for 60%

profile of v2, /device:TPU:9, one launch (start us, length us, event | category | flops | bytes accessed | tf_op | source)
XLA Modules:
  0.0 529.9 jit_solution(15652615635157930096)
XLA Ops:
  7.2 8.6 %dynamic-slice_bitcast_fusion = f32[768,3072]{1,0:T(8,128)} fusion(f32[1,768,6144]{2,1,0:T(8,128)} %param.7, s32[]{:T(128)S(6)} %select_n.59), kind=kLoop, calls=%fused_computation | loop fusion | bytes 18874372 | tf_op jit(solution)/shard_map/dynamic_slice | solution.py:457
  17.6 23.7 %all-gather = f32[768,256]{1,0:T(8,128)S(1)} all-gather(f32[192,256]{1,0:T(8,128)S(1)} %get-tuple-element.37), channel_id=2, replica_groups=mesh['leaf'=4,'prow'=4,'pcol'=2] {'prow'}, dimensions={0}, use_global_device_ids=true | all-gather | bytes 983040 | tf_op jit(solution)/shard_map/all_gather | solution.py:454
  42.4 1.5 subtract_bitcast_fusion
  45.5 31.9 %shard_map.76.refs_4_.parent = f32[1024,4096]{1,0:T(8,128)} custom-call(s32[1]{0:T(128)} %bitcast.4.first, f32[768,6144]{1,0:T(8,128)} %bitcast.29, s32[1,1,768]{2,1,0:T(1,128)} %get-tuple-element.42.row_links.own_links, s32[4,1,1,768]{3,2,1,0:T(1,128)} %get-tuple-element.44.col_links.own_links, f32[1024,4096]{1,0:T(8,128)} %bitcast.42), custom_call_target="tpu_custom_call" | custom-call | flops 22548578304 | bytes 42991616 | tf_op jit(solution)/shard_map/pallas_call | solution.py:312
  78.3 19.0 %shard_map.77 = (f32[1536,256]{1,0:T(8,128)}, f32[768,256]{1,0:T(8,128)}, bf16[768,256]{1,0:T(8,128)(2,1)}) custom-call(s32[1]{0:T(128)} %bitcast.refs_0_, f32[4,192,256]{2,1,0:T(8,128)} %bitcast.39, f32[4,192,256]{2,1,0:T(8,128)} %copy-done.21, f32[768,1536]{1,0:T(8,128)} %bitcast.43, f32[1024,4096]{1,0:T(8,128)} %shard_map.76.refs_4_.parent), custom_call_target="tpu_custom_call" | custom-call | flops 12800000000 | bytes 5898240 | tf_op jit(solution)/shard_map/pallas_call | solution.py:255
  98.1 31.8 %shard_map.78.refs_6_.total = f32[1024,4096]{1,0:T(8,128)} custom-call(s32[1]{0:T(128)} %constant.104.clone.1.first, f32[768,3072]{1,0:T(8,128)} %collective-permute-done.2.values, s32[1,1,768]{2,1,0:T(1,128)} %get-tuple-element.41.row_links.other_links, s32[4,1,1,768]{3,2,1,0:T(1,128)} %get-tuple-element.43.col_links.other_links, ...), custom_call_target="tpu_custom_call", output_to_operand_aliasing={{}: (4, {})} | custom-call | flops 22548578304 | bytes 42991616 | tf_op jit(solution)/shard_map/pallas_call | solution.py:312
  129.9 1.5 collective-permute-done.1.refs_2_
  132.6 44.4 %shard_map.79 = (f32[1536,512]{1,0:T(8,128)}, f32[768,512]{1,0:T(8,128)}, bf16[768,512]{1,0:T(8,128)(2,1)}) custom-call(s32[1]{0:T(128)} %bitcast.refs_0_, f32[4,192,512]{2,1,0:T(8,128)} %bitcast.48, f32[4,192,512]{2,1,0:T(8,128)} %copy-done.20, f32[1536,256]{1,0:T(8,128)} %get-tuple-element.15.refs_3_, f32[768,256]{1,0:T(8,128)} %get-tuple-element.16.refs_4_, ...), custom_call_target="tpu_custom_call" | custom-call | flops 25600000000 | bytes 11796480 | tf_op jit(solution)/shard_map/pallas_call | solution.py:255
  179.1 15.4 %collective-permute-done.3.refs_2_ = f32[2,192,512]{2,1,0:T(8,128)S(1)} collective-permute-done((f32[2,192,512]{2,1,0:T(8,128)S(1)}, f32[2,192,512]{2,1,0:T(8,128)S(1)}, u32[]{:S(2)}, u32[]{:S(2)}) %collective-permute-start.3) | collective-permute-done | bytes 786464 | tf_op jit(solution)/shard_map/ppermute | solution.py:432
  195.4 41.6 %shard_map.80 = (f32[768,512]{1,0:T(8,128)}, f32[768,512]{1,0:T(8,128)}, bf16[768,512]{1,0:T(8,128)(2,1)}) custom-call(s32[1]{0:T(128)} %bitcast.refs_0_, f32[2,192,512]{2,1,0:T(8,128)} %bitcast.37, f32[2,192,512]{2,1,0:T(8,128)} %copy-done.22, f32[1536,256]{1,0:T(8,128)} %get-tuple-element.15.refs_3_, f32[768,256]{1,0:T(8,128)} %get-tuple-element.16.refs_4_, ...), custom_call_target="tpu_custom_call" | custom-call | flops 25600000000 | bytes 7864320 | tf_op jit(solution)/shard_map/pallas_call | solution.py:255
  237.1 17.1 %all-gather.3 = f32[768,256]{1,0:T(8,128)S(1)} all-gather(f32[192,256]{1,0:T(8,128)S(1)} %get-tuple-element.38), channel_id=5, replica_groups=mesh['leaf'=4,'prow'=4,'pcol'=2] {'prow'}, dimensions={0}, use_global_device_ids=true | all-gather | bytes 983040 | tf_op jit(solution)/shard_map/all_gather | solution.py:454
  254.2 8.0 %collective-permute-start.17 = (bf16[768,256]{1,0:T(8,128)(2,1)S(1)}, bf16[768,256]{1,0:T(8,128)(2,1)S(1)}, u32[]{:S(2)}, u32[]{:S(2)}) collective-permute-start(bf16[768,256]{1,0:T(8,128)(2,1)S(1)} %copy-done.16), channel_id=1, source_target_pairs={{0,8},{8,0},{16,24},{24,16},{1,9},{9,1},{17,25},{25,17},{2,10},{10... | collective-permute-start | bytes 1179656 | tf_op jit(solution)/shard_map/ppermute | solution.py:423
  266.0 3.1 shard_map.85.rows
  269.1 2.4 constant_dynamic-slice_fusion
  274.5 23.0 %shard_map.81 = (f32[384,256]{1,0:T(8,128)}, f32[768,256]{1,0:T(8,128)}, bf16[768,256]{1,0:T(8,128)(2,1)}) custom-call(s32[1]{0:T(128)} %bitcast.refs_0_, f32[1,192,256]{2,1,0:T(8,128)} %copy-done.19, f32[1,192,256]{2,1,0:T(8,128)} %copy-done.25, f32[1536,256]{1,0:T(8,128)} %get-tuple-element.15.refs_3_, f32[768,256]{1,0:T(8,128)} %get-tuple-element.16.refs_4_, ...), custom_call_target="tpu_custom_call" | custom-call | flops 12800000000 | bytes 2949120 | tf_op jit(solution)/shard_map/pallas_call | solution.py:255
  297.7 14.7 %shard_map.86.total = f32[1024,4096]{1,0:T(8,128)} custom-call(s32[2]{0:T(128)} %fusion.places, bf16[1024,512]{1,0:T(8,128)(2,1)} %shard_map.85.rows, bf16[2,768,256]{2,1,0:T(8,128)(2,1)} %copy-done.3, bf16[2,768,256]{2,1,0:T(8,128)(2,1)} %collective-permute-done.20.other, ...), custom_call_target="tpu_custom_call", output_to_operand_aliasing={{}: (6, {})} | custom-call | flops 3758096384 | bytes 16777216 | tf_op jit(solution)/shard_map/pallas_call | solution.py:379
  313.7 2.6 maximum_bitcast_fusion
  316.4 3.4 constant_dynamic-slice_fusion.2
  321.5 14.1 %shard_map.87.total = f32[1024,4096]{1,0:T(8,128)} custom-call(s32[2]{0:T(128)} %fusion.1.places, bf16[1024,512]{1,0:T(8,128)(2,1)} %shard_map.85.rows, bf16[2,768,256]{2,1,0:T(8,128)(2,1)} %collective-permute-done.18.own, bf16[2,768,256]{2,1,0:T(8,128)(2,1)} %collective-permute-done.19.other, ...), custom_call_target="tpu_custom_call", output_to_operand_aliasing={{}: (6, {})} | custom-call | flops 3758096384 | bytes 16777216 | tf_op jit(solution)/shard_map/pallas_call | solution.py:379
  338.5 3.1 shard_map.82.rows
  341.6 4.5 shard_map.84.rows
  346.1 3.3 constant_dynamic-slice_fusion.4
  350.0 4.5 shard_map.83.rows
  354.5 1.5 constant_dynamic-slice_fusion.6
  358.0 17.4 %shard_map.88.total = f32[1024,4096]{1,0:T(8,128)} custom-call(s32[2]{0:T(128)} %fusion.places, bf16[1024,1024]{1,0:T(8,128)(2,1)} %shard_map.84.rows, bf16[2,768,512]{2,1,0:T(8,128)(2,1)} %copy-done, bf16[2,768,512]{2,1,0:T(8,128)(2,1)} %collective-permute-done.16.other, ...), custom_call_target="tpu_custom_call", output_to_operand_aliasing={{}: (6, {})} | custom-call | flops 7516192768 | bytes 16777216 | tf_op jit(solution)/shard_map/pallas_call | solution.py:379
  375.4 30.3 %collective-permute-done.14.own = bf16[2,768,512]{2,1,0:T(8,128)(2,1)} collective-permute-done((bf16[2,768,512]{2,1,0:T(8,128)(2,1)S(1)}, bf16[2,768,512]{2,1,0:T(8,128)(2,1)}, u32[]{:S(2)}, u32[]{:S(2)}) %collective-permute-start.14) | collective-permute-done | bytes 1572896 | tf_op jit(solution)/shard_map/ppermute | solution.py:432
  407.5 17.3 %shard_map.89.total = f32[1024,4096]{1,0:T(8,128)} custom-call(s32[2]{0:T(128)} %fusion.1.places, bf16[1024,1024]{1,0:T(8,128)(2,1)} %shard_map.84.rows, bf16[2,768,512]{2,1,0:T(8,128)(2,1)} %collective-permute-done.14.own, bf16[2,768,512]{2,1,0:T(8,128)(2,1)} %collective-permute-done.15.other, ...), custom_call_target="tpu_custom_call", output_to_operand_aliasing={{}: (6, {})} | custom-call | flops 7516192768 | bytes 16777216 | tf_op jit(solution)/shard_map/pallas_call | solution.py:379
  425.8 17.3 %shard_map.90.total = f32[1024,4096]{1,0:T(8,128)} custom-call(s32[2]{0:T(128)} %fusion.places, bf16[1024,1024]{1,0:T(8,128)(2,1)} %shard_map.83.rows, bf16[2,768,512]{2,1,0:T(8,128)(2,1)} %copy-done.1, bf16[2,768,512]{2,1,0:T(8,128)(2,1)} %collective-permute-done.12.other, ...), custom_call_target="tpu_custom_call", output_to_operand_aliasing={{}: (6, {})} | custom-call | flops 7516192768 | bytes 16777216 | tf_op jit(solution)/shard_map/pallas_call | solution.py:379
  443.1 30.0 %collective-permute-done.10.own = bf16[2,768,512]{2,1,0:T(8,128)(2,1)S(1)} collective-permute-done((bf16[2,768,512]{2,1,0:T(8,128)(2,1)S(1)}, bf16[2,768,512]{2,1,0:T(8,128)(2,1)S(1)}, u32[]{:S(2)}, u32[]{:S(2)}) %collective-permute-start.10) | collective-permute-done | bytes 1572896 | tf_op jit(solution)/shard_map/ppermute | solution.py:432
  475.4 17.3 %shard_map.91.total = f32[1024,4096]{1,0:T(8,128)} custom-call(s32[2]{0:T(128)} %fusion.1.places, bf16[1024,1024]{1,0:T(8,128)(2,1)} %shard_map.83.rows, bf16[2,768,512]{2,1,0:T(8,128)(2,1)} %copy-done.8, bf16[2,768,512]{2,1,0:T(8,128)(2,1)} %copy-done.7, s32[4,1,1,768]{3,2,1,0:T(1,128)} %get-tuple-element.44.col_links.own_links, ...), custom_call_target="tpu_custom_call", output_to_operand_aliasing={{}: (6, {})} | custom-call | flops 7516192768 | bytes 16777216 | tf_op jit(solution)/shard_map/pallas_call | solution.py:379
  493.7 14.1 %shard_map.92.total = f32[1024,4096]{1,0:T(8,128)} custom-call(s32[2]{0:T(128)} %fusion.places, bf16[1024,512]{1,0:T(8,128)(2,1)} %shard_map.82.rows, bf16[2,768,256]{2,1,0:T(8,128)(2,1)} %copy-done.2, bf16[2,768,256]{2,1,0:T(8,128)(2,1)} %copy-done.15, s32[4,1,1,768]{3,2,1,0:T(1,128)} %get-tuple-element.44.col_links.own_links, ...), custom_call_target="tpu_custom_call", output_to_operand_aliasing={{}: (6, {})} | custom-call | flops 3758096384 | bytes 16777216 | tf_op jit(solution)/shard_map/pallas_call | solution.py:379
  508.7 14.1 %shard_map.93 = f32[1024,4096]{1,0:T(8,128)} custom-call(s32[2]{0:T(128)} %fusion.1.places, bf16[1024,512]{1,0:T(8,128)(2,1)} %shard_map.82.rows, bf16[2,768,256]{2,1,0:T(8,128)(2,1)} %collective-permute-done.6.own, bf16[2,768,256]{2,1,0:T(8,128)(2,1)} %copy-done.14, ...), custom_call_target="tpu_custom_call", output_to_operand_aliasing={{}: (6, {})} | custom-call | flops 3758096384 | bytes 16777216 | tf_op jit(solution)/shard_map/pallas_call | solution.py:379
  (121 shorter events, 32.7 us)
Async XLA Ops:
  7.2 90.4 %all-gather.15.cloned.1.call-start = ((), (), s32[]{:S(2)}) async-start(), calls=%async_computation | async-start | bytes 1966080 | tf_op jit(solution)/shard_map/all_gather | solution.py:454
  15.9 82.3 %collective-permute-start.2 = (f32[768,3072]{1,0:T(8,128)}, f32[768,3072]{1,0:T(8,128)}, u32[]{:S(2)}, u32[]{:S(2)}) collective-permute-start(f32[768,3072]{1,0:T(8,128)} %dynamic-slice_bitcast_fusion), channel_id=1, source_target_pairs={{0,8},{8,0},{16,24},{24,16},{1,9},{9,1},{17,25},{25,17},{2,10},{10... | collective-permute-start | bytes 28311560 | tf_op jit(solution)/shard_map/ppermute | solution.py:423
  17.5 159.8 %all-gather.17.cloned.1.call-start = ((), (), s32[]{:S(2)}) async-start(), calls=%async_computation.1 | async-start | bytes 1966080 | tf_op jit(solution)/shard_map/all_gather | solution.py:454
  41.2 36.1 %copy-start.13 = (f32[768,256]{1,0:T(8,128)}, f32[768,256]{1,0:T(8,128)S(1)}, u32[]{:S(2)}) copy-start(f32[768,256]{1,0:T(8,128)S(1)} %all-gather) | copy-start | bytes 2359300
  41.2 36.1 %collective-permute-start = (f32[4,192,256]{2,1,0:T(8,128)S(1)}, f32[4,192,256]{2,1,0:T(8,128)S(1)}, u32[]{:S(2)}, u32[]{:S(2)}) collective-permute-start(f32[4,192,256]{2,1,0:T(8,128)S(1)} %bitcast.38), channel_id=1, source_target_pairs={{0,1},{1,0},{2,3},{3,2},{4,5},{5,4},{6,7},{7,6},{8,9},{9,8},{10,11... | collective-permute-start | bytes 2359304 | tf_op jit(solution)/shard_map/ppermute | solution.py:432
  42.3 226.8 %all-gather.25.cloned.1.call-start = ((), (), s32[]{:S(2)}) async-start(), calls=%async_computation.5 | async-start | bytes 1966080 | tf_op jit(solution)/shard_map/all_gather | solution.py:472
  97.3 219.0 %all-gather.23.cloned.1.call-start = ((), (), s32[]{:S(2)}) async-start(), calls=%async_computation.4 | async-start | bytes 3932160 | tf_op jit(solution)/shard_map/all_gather | solution.py:472
  97.6 33.9 %collective-permute-start.1 = (f32[4,192,512]{2,1,0:T(8,128)}, f32[4,192,512]{2,1,0:T(8,128)S(1)}, u32[]{:S(2)}, u32[]{:S(2)}) collective-permute-start(f32[4,192,512]{2,1,0:T(8,128)} %bitcast.47), channel_id=1, source_target_pairs={{0,1},{1,0},{2,3},{3,2},{4,5},{5,4},{6,7},{7,6},{8,9},{9,8},{10,11... | collective-permute-start | bytes 4718600 | tf_op jit(solution)/shard_map/ppermute | solution.py:432
  177.0 169.0 %all-gather.21.cloned.1.call-start = ((), (), s32[]{:S(2)}) async-start(), calls=%async_computation.3 | async-start | bytes 3932160 | tf_op jit(solution)/shard_map/all_gather | solution.py:472
  178.5 15.9 %collective-permute-start.3 = (f32[2,192,512]{2,1,0:T(8,128)S(1)}, f32[2,192,512]{2,1,0:T(8,128)S(1)}, u32[]{:S(2)}, u32[]{:S(2)}) collective-permute-start(f32[2,192,512]{2,1,0:T(8,128)S(1)} %bitcast.36), channel_id=1, source_target_pairs={{0,1},{1,0},{2,3},{3,2},{4,5},{5,4},{6,7},{7,6},{8,9},{9,8},{10,11... | collective-permute-start | bytes 2359304 | tf_op jit(solution)/shard_map/ppermute | solution.py:432
  237.0 17.2 %copy-start.16 = (bf16[768,256]{1,0:T(8,128)(2,1)S(1)}, bf16[768,256]{1,0:T(8,128)(2,1)}, u32[]{:S(2)}) copy-start(bf16[768,256]{1,0:T(8,128)(2,1)} %get-tuple-element.26.own) | copy-start | bytes 1179652
  237.0 117.5 %all-gather.19.cloned.1.call-start = ((), (), s32[]{:S(2)}) async-start(), calls=%async_computation.2 | async-start | bytes 1966080 | tf_op jit(solution)/shard_map/all_gather | solution.py:472
  254.2 11.1 %collective-permute-start.17 = (bf16[768,256]{1,0:T(8,128)(2,1)S(1)}, bf16[768,256]{1,0:T(8,128)(2,1)S(1)}, u32[]{:S(2)}, u32[]{:S(2)}) collective-permute-start(bf16[768,256]{1,0:T(8,128)(2,1)S(1)} %copy-done.16), channel_id=1, source_target_pairs={{0,8},{8,0},{16,24},{24,16},{1,9},{9,1},{17,25},{25,17},{2,10},{10... | collective-permute-start | bytes 1179656 | tf_op jit(solution)/shard_map/ppermute | solution.py:423
  262.2 11.7 %collective-permute-start.4 = (f32[1,192,256]{2,1,0:T(8,128)S(1)}, f32[1,192,256]{2,1,0:T(8,128)S(1)}, u32[]{:S(2)}, u32[]{:S(2)}) collective-permute-start(f32[1,192,256]{2,1,0:T(8,128)S(1)} %slice_bitcast_fusion.refs_1_), channel_id=1, source_target_pairs={{0,1},{1,0},{2,3},{3,2},{4,5},{5,4},{6,7},{7,6},{8,9},{9,8},{10,11... | collective-permute-start | bytes 589832 | tf_op jit(solution)/shard_map/ppermute | solution.py:432
  271.4 26.1 %copy-start.3 = (bf16[2,768,256]{2,1,0:T(8,128)(2,1)}, bf16[2,768,256]{2,1,0:T(8,128)(2,1)S(1)}, u32[]{:S(2)}) copy-start(bf16[2,768,256]{2,1,0:T(8,128)(2,1)S(1)} %get-tuple-element.32.own) | copy-start | bytes 2359300
  271.4 26.2 %collective-permute-start.20 = (bf16[2,768,256]{2,1,0:T(8,128)(2,1)}, bf16[2,768,256]{2,1,0:T(8,128)(2,1)}, u32[]{:S(2)}, u32[]{:S(2)}) collective-permute-start(bf16[2,768,256]{2,1,0:T(8,128)(2,1)} %get-tuple-element.31), channel_id=1, source_target_pairs={{0,8},{1,9},{2,10},{3,11},{4,12},{5,13},{6,14},{7,15},{8,0},{9,1},... | collective-permute-start | bytes 2359304 | tf_op jit(solution)/shard_map/ppermute | solution.py:432
  271.7 49.8 %collective-permute-start.19 = (bf16[2,768,256]{2,1,0:T(8,128)(2,1)}, bf16[2,768,256]{2,1,0:T(8,128)(2,1)}, u32[]{:S(2)}, u32[]{:S(2)}) collective-permute-start(bf16[2,768,256]{2,1,0:T(8,128)(2,1)} %get-tuple-element.31), channel_id=1, source_target_pairs={{0,9},{1,8},{2,11},{3,10},{4,13},{5,12},{6,15},{7,14},{8,1},{9,0},... | collective-permute-start | bytes 2359304 | tf_op jit(solution)/shard_map/ppermute | solution.py:432
  272.4 48.7 %collective-permute-start.18 = (bf16[2,768,256]{2,1,0:T(8,128)(2,1)S(1)}, bf16[2,768,256]{2,1,0:T(8,128)(2,1)}, u32[]{:S(2)}, u32[]{:S(2)}) collective-permute-start(bf16[2,768,256]{2,1,0:T(8,128)(2,1)S(1)} %get-tuple-element.32.own), channel_id=1, source_target_pairs={{0,1},{1,0},{2,3},{3,2},{4,5},{5,4},{6,7},{7,6},{8,9},{9,8},{10,11... | collective-permute-start | bytes 2359304 | tf_op jit(solution)/shard_map/ppermute | solution.py:432
  273.3 68.3 %collective-permute-start.13 = (bf16[768,512]{1,0:T(8,128)(2,1)}, bf16[768,512]{1,0:T(8,128)(2,1)}, u32[]{:S(2)}, u32[]{:S(2)}) collective-permute-start(bf16[768,512]{1,0:T(8,128)(2,1)} %get-tuple-element.25.own), channel_id=1, source_target_pairs={{0,8},{8,0},{16,24},{24,16},{1,9},{9,1},{17,25},{25,17},{2,10},{10... | collective-permute-start | bytes 2359304 | tf_op jit(solution)/shard_map/ppermute | solution.py:423
  273.9 76.2 %collective-permute-start.9 = (bf16[768,512]{1,0:T(8,128)(2,1)}, bf16[768,512]{1,0:T(8,128)(2,1)}, u32[]{:S(2)}, u32[]{:S(2)}) collective-permute-start(bf16[768,512]{1,0:T(8,128)(2,1)} %get-tuple-element.24.own), channel_id=1, source_target_pairs={{0,8},{8,0},{16,24},{24,16},{1,9},{9,1},{17,25},{25,17},{2,10},{10... | collective-permute-start | bytes 2359304 | tf_op jit(solution)/shard_map/ppermute | solution.py:423
  319.8 16.6 %copy-start = (bf16[2,768,512]{2,1,0:T(8,128)(2,1)}, bf16[2,768,512]{2,1,0:T(8,128)(2,1)S(1)}, u32[]{:S(2)}) copy-start(bf16[2,768,512]{2,1,0:T(8,128)(2,1)S(1)} %get-tuple-element.28.own) | copy-start | bytes 4718596
  319.8 37.2 %collective-permute-start.16 = (bf16[2,768,512]{2,1,0:T(8,128)(2,1)}, bf16[2,768,512]{2,1,0:T(8,128)(2,1)}, u32[]{:S(2)}, u32[]{:S(2)}) collective-permute-start(bf16[2,768,512]{2,1,0:T(8,128)(2,1)} %get-tuple-element.27), channel_id=1, source_target_pairs={{0,8},{1,9},{2,10},{3,11},{4,12},{5,13},{6,14},{7,15},{8,0},{9,1},... | collective-permute-start | bytes 4718600 | tf_op jit(solution)/shard_map/ppermute | solution.py:432
  321.1 15.2 %collective-permute-start.5 = (bf16[768,256]{1,0:T(8,128)(2,1)S(1)}, bf16[768,256]{1,0:T(8,128)(2,1)S(1)}, u32[]{:S(2)}, u32[]{:S(2)}) collective-permute-start(bf16[768,256]{1,0:T(8,128)(2,1)S(1)} %copy-done.17), channel_id=1, source_target_pairs={{0,8},{8,0},{16,24},{24,16},{1,9},{9,1},{17,25},{25,17},{2,10},{10... | collective-permute-start | bytes 1179656 | tf_op jit(solution)/shard_map/ppermute | solution.py:423
  335.7 71.4 %collective-permute-start.15 = (bf16[2,768,512]{2,1,0:T(8,128)(2,1)}, bf16[2,768,512]{2,1,0:T(8,128)(2,1)}, u32[]{:S(2)}, u32[]{:S(2)}) collective-permute-start(bf16[2,768,512]{2,1,0:T(8,128)(2,1)} %get-tuple-element.27), channel_id=1, source_target_pairs={{0,9},{1,8},{2,11},{3,10},{4,13},{5,12},{6,15},{7,14},{8,1},{9,0},... | collective-permute-start | bytes 4718600 | tf_op jit(solution)/shard_map/ppermute | solution.py:432
  336.4 69.4 %collective-permute-start.14 = (bf16[2,768,512]{2,1,0:T(8,128)(2,1)S(1)}, bf16[2,768,512]{2,1,0:T(8,128)(2,1)}, u32[]{:S(2)}, u32[]{:S(2)}) collective-permute-start(bf16[2,768,512]{2,1,0:T(8,128)(2,1)S(1)} %get-tuple-element.28.own), channel_id=1, source_target_pairs={{0,1},{1,0},{2,3},{3,2},{4,5},{5,4},{6,7},{7,6},{8,9},{9,8},{10,11... | collective-permute-start | bytes 4718600 | tf_op jit(solution)/shard_map/ppermute | solution.py:432
  349.4 75.4 %collective-permute-start.12 = (bf16[2,768,512]{2,1,0:T(8,128)(2,1)}, bf16[2,768,512]{2,1,0:T(8,128)(2,1)}, u32[]{:S(2)}, u32[]{:S(2)}) collective-permute-start(bf16[2,768,512]{2,1,0:T(8,128)(2,1)} %get-tuple-element.29), channel_id=1, source_target_pairs={{0,8},{1,9},{2,10},{3,11},{4,12},{5,13},{6,14},{7,15},{8,0},{9,1},... | collective-permute-start | bytes 4718600 | tf_op jit(solution)/shard_map/ppermute | solution.py:432
  356.0 68.8 %copy-start.2 = (bf16[2,768,256]{2,1,0:T(8,128)(2,1)}, bf16[2,768,256]{2,1,0:T(8,128)(2,1)S(1)}, u32[]{:S(2)}) copy-start(bf16[2,768,256]{2,1,0:T(8,128)(2,1)S(1)} %get-tuple-element.34.own) | copy-start | bytes 2359300
  356.0 117.1 %collective-permute-start.11 = (bf16[2,768,512]{2,1,0:T(8,128)(2,1)}, bf16[2,768,512]{2,1,0:T(8,128)(2,1)S(1)}, u32[]{:S(2)}, u32[]{:S(2)}) collective-permute-start(bf16[2,768,512]{2,1,0:T(8,128)(2,1)} %get-tuple-element.29), channel_id=1, source_target_pairs={{0,9},{1,8},{2,11},{3,10},{4,13},{5,12},{6,15},{7,14},{8,1},{9,0},... | collective-permute-start | bytes 4718600 | tf_op jit(solution)/shard_map/ppermute | solution.py:432
  357.0 116.0 %collective-permute-start.10 = (bf16[2,768,512]{2,1,0:T(8,128)(2,1)S(1)}, bf16[2,768,512]{2,1,0:T(8,128)(2,1)S(1)}, u32[]{:S(2)}, u32[]{:S(2)}) collective-permute-start(bf16[2,768,512]{2,1,0:T(8,128)(2,1)S(1)} %get-tuple-element.30.own), channel_id=1, source_target_pairs={{0,1},{1,0},{2,3},{3,2},{4,5},{5,4},{6,7},{7,6},{8,9},{9,8},{10,11... | collective-permute-start | bytes 4718600 | tf_op jit(solution)/shard_map/ppermute | solution.py:432
  405.8 86.9 %collective-permute-start.8 = (bf16[2,768,256]{2,1,0:T(8,128)(2,1)S(1)}, bf16[2,768,256]{2,1,0:T(8,128)(2,1)S(1)}, u32[]{:S(2)}, u32[]{:S(2)}) collective-permute-start(bf16[2,768,256]{2,1,0:T(8,128)(2,1)S(1)} %get-tuple-element.33), channel_id=1, source_target_pairs={{0,8},{1,9},{2,10},{3,11},{4,12},{5,13},{6,14},{7,15},{8,0},{9,1},... | collective-permute-start | bytes 2359304 | tf_op jit(solution)/shard_map/ppermute | solution.py:432
  407.1 100.7 %collective-permute-start.7 = (bf16[2,768,256]{2,1,0:T(8,128)(2,1)S(1)}, bf16[2,768,256]{2,1,0:T(8,128)(2,1)S(1)}, u32[]{:S(2)}, u32[]{:S(2)}) collective-permute-start(bf16[2,768,256]{2,1,0:T(8,128)(2,1)S(1)} %get-tuple-element.33), channel_id=1, source_target_pairs={{0,9},{1,8},{2,11},{3,10},{4,13},{5,12},{6,15},{7,14},{8,1},{9,0},... | collective-permute-start | bytes 2359304 | tf_op jit(solution)/shard_map/ppermute | solution.py:432
  424.8 83.0 %collective-permute-start.6 = (bf16[2,768,256]{2,1,0:T(8,128)(2,1)S(1)}, bf16[2,768,256]{2,1,0:T(8,128)(2,1)}, u32[]{:S(2)}, u32[]{:S(2)}) collective-permute-start(bf16[2,768,256]{2,1,0:T(8,128)(2,1)S(1)} %get-tuple-element.34.own), channel_id=1, source_target_pairs={{0,1},{1,0},{2,3},{3,2},{4,5},{5,4},{6,7},{7,6},{8,9},{9,8},{10,11... | collective-permute-start | bytes 2359304 | tf_op jit(solution)/shard_map/ppermute | solution.py:432
  (21 other events, 130.2 us)
Sparse Core Ops, SparseCore 0:
  17.6 43.8 all-gather.14
  63.0 34.8 all-gather.16
  99.5 36.4 all-gather.24
  177.2 64.8 all-gather.22
  243.4 65.3 all-gather.20
  310.2 36.4 all-gather.18

commit v3 on v2

--- a/solution.py
+++ b/solution.py
@@ -50,6 +50,11 @@
 
 def spread_sub(x, sub):
     return jnp.broadcast_to(x[sub:sub + 1, :], (SUBS, LANES))
+
+
+def inverse_of(x):
+    guess = pl.reciprocal(x, approx=True)
+    return guess * (2.0 - x * guess)
 
 
 def factor_square(square):
@@ -78,33 +83,31 @@
             ahead = jnp.where(inside, 0.0, ahead)
         scales, steps = [], []
         for i in range(SUBS):
-            scale = lax.rsqrt(d[i][i])
+            scale = inverse_of(d[i][i])
             scales.append(scale)
             step = [d[i][k] * scale if k > i else None for k in range(SUBS)]
             steps.append(step)
-            rows[i] = rows[i] * scale
-            if follow:
-                beside[i] = beside[i] * scale
-                ahead = ahead - beside[i] * rows[i]
             for k in range(i + 1, SUBS):
                 for m in range(k, SUBS):
-                    d[k][m] = d[k][m] - step[k] * step[m]
+                    d[k][m] = d[k][m] - step[k] * d[i][m]
+            for k in range(i + 1, SUBS):
                 rows[k] = rows[k] - step[k] * rows[i]
                 if follow:
                     beside[k] = beside[k] - step[k] * beside[i]
-        whole = rows[0]
+            if follow:
+                ahead = ahead - (beside[i] * scale) * rows[i]
+        whole = rows[0] * lax.rsqrt(d[0][0])
         for i in range(1, SUBS):
-            whole = jnp.where(sub == i, rows[i], whole)
+            whole = jnp.where(sub == i, rows[i] * lax.rsqrt(d[i][i]), whole)
         inverses.append(whole)
         if follow:
             state[b + 1] = ahead
         if b + 2 < last:
             back = [None] * SUBS
             for i in reversed(range(SUBS)):
-                total = rows[i]
+                back[i] = rows[i] * scales[i]
                 for k in range(i + 1, SUBS):
-                    total = total - steps[i][k] * back[k]
-                back[i] = total * scales[i]
+                    back[i] = back[i] - steps[i][k] * back[k]
             for r in range(b + 2, last):
                 below = state[r]
                 left = [spread_lane(below, first + k) for k in range(SUBS)]
@@ -139,14 +142,16 @@
     return next(t for t in (256, 128, 64, 32, 16, 8) if rows % t == 0)
 
 
-def panel_kernel(first, base, bases, pcols, *refs):
+def panel_kernel(first, base, bases, pcols, turned, *refs):
     refs = list(refs)
-    across, shares, refs = refs[0], refs[1:1 + pcols], refs[1 + pcols:]
+    place, shares, refs = refs[0], refs[1:1 + pcols], refs[1 + pcols:]
     before = len(bases)
     earlier = [(refs[2 * q], refs[2 * q + 1]) for q in range(before)]
     refs = refs[2 * before:]
-    lower_in, _, pivot, lower, rounded, tops = refs[:6]
-    crowns = refs[6:]
+    waits = len(refs) - 4 - before
+    lower_in = refs[0]
+    pivot, lower, rounded, tops = refs[waits:waits + 4]
+    crowns = refs[waits + 4:]
     width = pivot.shape[1]
     count = width // LANES
     skip = first - base
@@ -157,11 +162,12 @@
             crowns[q][t * LANES:(t + 1) * LANES, :] = right_parts(
                 earlier[q][0][at:at + LANES, :]
             )
-    share_rows = shares[0].shape[1]
+    prows, share_rows = shares[0].shape[:2]
     for apart in range(pcols):
-        source = lax.rem(across[0] - apart + pcols, pcols)
-        for r in range(shares[apart].shape[0]):
-            at = pl.multiple_of((r * pcols + source) * share_rows, 8)
+        source = lax.rem(place[1] - apart + pcols, pcols)
+        for r in range(prows):
+            line = lax.rem(place[0] - r + prows, prows) if turned else r
+            at = pl.multiple_of((line * pcols + source) * share_rows, 8)
             pivot[pl.ds(at, share_rows), :] = shares[apart][r]
     pltpu.sync_copy(lower_in.at[:, first:first + width], lower)
 
@@ -243,7 +249,7 @@
         rounded[here, :] = lower[here, :].astype(bf16)
 
 
-def factor_panel(first, across, shares, lower, earlier, after):
+def factor_panel(first, place, shares, turned, lower, earlier, after):
     prows, share_rows, width = shares[0].shape
     rows = len(shares) * prows * share_rows
     order = lower.shape[1]
@@ -253,7 +259,7 @@
     anywhere = pl.BlockSpec(memory_space=pl.ANY)
     bases = [order - past.shape[0] for past, _ in earlier]
     return pl.pallas_call(
-        lambda *refs: panel_kernel(first, base, bases, len(shares), *refs),
+        lambda *refs: panel_kernel(first, base, bases, len(shares), turned, *refs),
         out_shape=(
             jax.ShapeDtypeStruct((rows, width), f32),
             jax.ShapeDtypeStruct((lower.shape[0], width), f32),
@@ -261,7 +267,7 @@
         ),
         in_specs=[pl.BlockSpec(memory_space=pltpu.SMEM)]
         + [in_vmem] * (len(shares) + len(flat))
-        + [anywhere] * 2,
+        + [anywhere] * (1 + len(after)),
         out_specs=[in_vmem] * 3,
         scratch_shapes=[pltpu.VMEM((width, 3 * LANES), bf16)]
         + [pltpu.VMEM((width, 3 * past.shape[1]), bf16) for past, _ in earlier],
@@ -271,7 +277,7 @@
             bytes_accessed=10 * width * (rows + lower.shape[0]),
             transcendentals=0,
         ),
-    )(across, *shares, *flat, lower, after)
+    )(place, *shares, *flat, lower, *after)
 
 
 def one_hot(links, window):
@@ -279,7 +285,12 @@
     return (places == links).astype(bf16)
 
 
-def rest_kernel(first, values, row_links, col_links, parent, out, table, placed):
+def rest_kernel(first, values, *refs):
+    if len(refs) == 8:
+        crossing, row_links, col_links, parent, out, leaving, table, placed = refs
+        leaving[...] = crossing[...]
+    else:
+        row_links, col_links, parent, out, table, placed = refs
     window = out.shape[0]
     rows = values.shape[0]
 
@@ -295,46 +306,51 @@
         block, area = slice(i * rows, (i + 1) * rows), slice(i * window, (i + 1) * window)
         placed[:rows, area] = nt(top[:, block], spread).astype(bf16)
         placed[rows:, area] = nt(low[:, block], spread).astype(bf16)
-    tile = largest_tile(window)
-
-    @pl.loop(0, window // tile)
+    tile = largest_tile(out.shape[1])
+
+    @pl.loop(0, out.shape[1] // tile)
     def _(t):
         here = pl.ds(pl.multiple_of(t * tile, tile), tile)
-        out[here, :] = parent[here, :] + nn(table[here, :], placed[...])
-
-
-def add_rest(parent, values, half, row_links, col_links, in_place):
+        out[:, here] = parent[:, here] + nn(table[...], placed[:, here])
+
+
+def add_rest(parent, values, half, row_links, col_links, whole):
     window = parent.shape[0]
     rows = values.shape[0]
     group = LANES // math.gcd(LANES, rows)
     steps = parent.shape[1] // window // group
     area = pl.BlockSpec((window, group * window), lambda w, half: (0, w))
+    block = (rows, group * rows)
+    total = jax.ShapeDtypeStruct(parent.shape, f32)
+    crossing = [pl.BlockSpec(block, lambda w, half: (0, (1 - half[0]) * steps + w))]
+    leaving = pl.BlockSpec(block, lambda w, half: (0, w))
     return pl.pallas_call(
         rest_kernel,
-        out_shape=jax.ShapeDtypeStruct(parent.shape, f32),
+        out_shape=(total, jax.ShapeDtypeStruct((rows, values.shape[1] // 2), f32)) if whole else total,
         grid_spec=pltpu.PrefetchScalarGridSpec(
             num_scalar_prefetch=1,
             grid=(steps,),
-            in_specs=[
-                pl.BlockSpec((rows, group * rows), lambda w, half: (0, half[0] * steps + w)),
+            in_specs=[pl.BlockSpec(block, lambda w, half: (0, half[0] * steps + w))]
+            + (crossing if whole else [])
+            + [
                 pl.BlockSpec((1, 1, rows), lambda w, half: (0, 0, 0)),
                 pl.BlockSpec((group, 1, 1, rows), lambda w, half: (w, 0, 0, 0)),
                 area,
             ],
-            out_specs=area,
+            out_specs=(area, leaving) if whole else area,
             scratch_shapes=[
                 pltpu.VMEM((window, 2 * rows), bf16),
                 pltpu.VMEM((2 * rows, group * window), bf16),
             ],
         ),
-        input_output_aliases={4: 0} if in_place else {},
+        input_output_aliases={} if whole else {4: 0},
         compiler_params=pltpu.CompilerParams(vmem_limit_bytes=VMEM_LIMIT),
         cost_estimate=pl.CostEstimate(
             flops=4 * rows * parent.size + 4 * rows * rows * parent.shape[1],
             bytes_accessed=8 * parent.size + 4 * rows * rows * steps * group,
             transcendentals=0,
         ),
-    )(half, values, row_links, col_links, parent)
+    )(half, *([values] * (2 if whole else 1)), row_links, col_links, parent)
 
 
 def rows_kernel(own, other, own_links, other_links, out):
@@ -366,7 +382,9 @@
                 one_hot(links[0, 0], window), values[0]
             ).astype(bf16)
 
-    out[...] = total[...] - nt(rows[...], cols[...])
+    tile = out.shape[1]
+    here = pl.ds(pl.multiple_of(pl.program_id(1) * tile, tile), tile)
+    out[...] = total[...] - nt(rows[...], cols[here, :])
 
 
 def update_windows(total, rows, own, other, places, col_links):
@@ -375,7 +393,9 @@
     tile = largest_tile(window)
     block = pl.BlockSpec((1, children, width), lambda i, t, places: (i, 0, 0))
     link = pl.BlockSpec((1, 1, 1, children), lambda i, t, places: (places[i], 0, 0, 0))
-    area = pl.BlockSpec((tile, window), lambda i, t, places: (t, places[i]))
+    area = pl.BlockSpec(
+        (window, tile), lambda i, t, places: (0, places[i] * (window // tile) + t)
+    )
     return pl.pallas_call(
         update_kernel,
         out_shape=jax.ShapeDtypeStruct(total.shape, f32),
@@ -383,7 +403,7 @@
             num_scalar_prefetch=1,
             grid=(count, window // tile),
             in_specs=[
-                pl.BlockSpec((tile, 2 * width), lambda i, t, places: (t, 0)),
+                pl.BlockSpec((window, 2 * width), lambda i, t, places: (0, 0)),
                 block,
                 block,
                 link,
@@ -449,24 +469,38 @@
 
     widths = panel_widths(pivot_order)
     starts = [sum(widths[:p]) for p in range(len(widths))]
+    def along(value, step):
+        return lax.ppermute(value, "prow", [(r, (r + step) % prows) for r in range(prows)])
+
     column_blocks = []
-    for s, w in zip(starts, widths):
-        mine = lax.all_gather(pivot_rows[:, s:s + w], "prow", axis=0)[s // (rows_here * pcols):]
+    for p, (s, w) in enumerate(zip(starts, widths)):
+        mine = pivot_rows[:, s:s + w]
+        if p == 0:
+            mine = jnp.stack([mine] + [along(mine, step) for step in range(1, prows)])
+        else:
+            mine = lax.all_gather(mine, "prow", axis=0)[s // (rows_here * pcols):]
         column_blocks.append([mine] + [to_cols(mine, apart, 0) for apart in range(1, pcols)])
 
-    leaving = lax.dynamic_slice_in_dim(rest_rows, (1 - side) * child_half, child_half, 1)
-    arrived = to_sibling(leaving)
     half = side.astype(jnp.int32).reshape(1)
-    start_total = add_rest(parent_rows, rest_rows, half, own_row_links, own_col_links, False)
+    start_total, leaving = add_rest(
+        parent_rows, rest_rows, half, own_row_links, own_col_links, True
+    )
     total = add_rest(
-        start_total, arrived, jnp.zeros((1,), jnp.int32), other_row_links, other_col_links, True
+        start_total,
+        to_sibling(leaving),
+        jnp.zeros((1,), jnp.int32),
+        other_row_links,
+        other_col_links,
+        False,
     )
 
     done, panels = [], []
-    across_one = across.astype(jnp.int32).reshape(1)
+    place = jnp.stack([lax.axis_index("prow"), across]).astype(jnp.int32)
     for p, (s, shares) in enumerate(zip(starts, column_blocks)):
-        wait_for = (start_total, total)[p] if p < 2 else done[-1][0]
-        pivot, lower, rounded = factor_panel(s, across_one, shares, lower_rows, done, wait_for)
+        waits = [(start_total,), (total,)][p] if p < 2 else panels[p - 2][2:]
+        if 0 < p < len(starts) - 1:
+            waits = waits + (column_blocks[p + 1][0],)
+        pivot, lower, rounded = factor_panel(s, place, shares, p == 0, lower_rows, done, waits)
         done.append((pivot, lower))
         other = to_sibling(rounded)
         line = lax.all_gather(rounded, "prow", axis=0)

time: 541 us -> 562 us (1.039)
  waiting for transfers between devices: 77.4 us -> 116 us
  blocking collectives: 40.8 us -> 22.4 us
  Pallas kernels: 333 us -> 342 us
  local copies, waits for them, and re-layouts: 34.6 us -> 27.9 us
    ppermute x0 -> x3, waiting for transfers between devices: none -> 34.5 us  [along(): lax.ppermute(value, 'prow', [(r, (r + step) % prows) for r in range(prows)])]
    all_gather x2 -> x1, blocking collectives: 40.8 us -> 22.4 us  [local(): mine = lax.all_gather(mine, 'prow', axis=0)[s // (rows_here * pcols):]]
    dynamic_slice x1 -> x0, local copies, waits for them, and re-layouts: 8.62 us -> none  [local(): lax.dynamic_slice_in_dim(rest_rows, (1 - side) * child_half, child_half, 1)]
    ppermute x5, starting transfers between devices: 9.73 us -> 1.69 us  [to_sibling(): return lax.ppermute(value, 'leaf', [(g, g ^ 1) for g in range(leaves)])]
  transfers between devices with their start and end apart: 27 -> 30, of which waited for: 4 -> 9; matrix products, arithmetic and copies ran while one was open for 4% -> 4% of each run, Pallas kernels for 60% -> 53%
where the time goes in v3:
time: 562 us; the launch traced here: 552 us
  Pallas kernels  342 us (61%)
  waiting for transfers between devices  116 us (21%)
  local copies, waits for them, and re-layouts  27.9 us (5%)
  blocking collectives  22.4 us (4%)
  starting transfers between devices  22.2 us (4%)
  between operations  14.6 us (3%)
  other arithmetic  7.66 us (1%)
    pallas_call x4, Pallas kernels, factor_panel(): pl.pallas_call(lambda *refs: panel_kernel(first, base, bases, len(shares)...  134 us
    pallas_call x8, Pallas kernels, update_windows(): pl.pallas_call(update_kernel, out_shape=jax.ShapeDtypeStruct(total.shape,...  126 us
    ppermute x16, waiting for transfers between devices, to_cols(): return lax.ppermute(value, ('leaf',) + ROWS, pairs)  76.6 us
    pallas_call x2, Pallas kernels, add_rest(): pl.pallas_call(rest_kernel, out_shape=(total, jax.ShapeDtypeStruct((rows,...  66.6 us
    ppermute x3, waiting for transfers between devices, along(): lax.ppermute(value, 'prow', [(r, (r + step) % prows) for r in range(prows)])  34.5 us
    all_gather x1, blocking collectives, local(): mine = lax.all_gather(mine, 'prow', axis=0)[s // (rows_here * pcols):]  22.4 us
    ppermute x16, starting transfers between devices, to_cols(): return lax.ppermute(value, ('leaf',) + ROWS, pairs)  16.3 us
    pallas_call x4, Pallas kernels, spread_rows(): pl.pallas_call(rows_kernel, out_shape=jax.ShapeDtypeStruct((window, 2 * o...  15.4 us
  transfers between devices with their start and end apart: 30, of which 9 were waited for; matrix products, arithmetic and copies ran while one was open for 4% of the time, Pallas kernels for 53%

profile of v3, /device:TPU:9, one launch (start us, length us, event | category | flops | bytes accessed | tf_op | source)
XLA Modules:
  0.0 552.4 jit_solution(16532823164719969560)
XLA Ops:
  10.4 34.6 %shard_map.76 = (f32[1024,4096]{1,0:T(8,128)}, f32[768,3072]{1,0:T(8,128)}) custom-call(s32[1]{0:T(128)} %bitcast.8.first, f32[768,6144]{1,0:T(8,128)} %bitcast.46, f32[768,6144]{1,0:T(8,128)} %bitcast.47, s32[1,1,768]{2,1,0:T(1,128)} %get-tuple-element.47.refs_1_.own_links, s32[4,1,1,768]{3,2,1,0:T(1,128)} %get-tuple-element.49.refs_2_.own_links, ...), custom_call_target="tpu_custom_call" | custom-call | flops 22548578304 | bytes 42991616 | tf_op jit(solution)/shard_map/pallas_call | solution.py:327
  51.4 2.8 collective-permute-done
  54.1 22.9 %collective-permute-done.1 = f32[192,256]{1,0:T(8,128)S(1)} collective-permute-done((f32[192,256]{1,0:T(8,128)S(1)}, f32[192,256]{1,0:T(8,128)S(1)}, u32[]{:S(2)}, u32[]{:S(2)}) %collective-permute-start.1) | collective-permute-done | bytes 196640 | tf_op jit(solution)/shard_map/ppermute | solution.py:473
  77.1 8.8 %collective-permute-done.2 = f32[192,256]{1,0:T(8,128)S(1)} collective-permute-done((f32[192,256]{1,0:T(8,128)S(1)}, f32[192,256]{1,0:T(8,128)S(1)}, u32[]{:S(2)}, u32[]{:S(2)}) %collective-permute-start.2) | collective-permute-done | bytes 196640 | tf_op jit(solution)/shard_map/ppermute | solution.py:473
  87.8 16.8 %collective-permute-done.3.refs_2_ = f32[4,192,256]{2,1,0:T(8,128)S(1)} collective-permute-done((f32[4,192,256]{2,1,0:T(8,128)S(1)}, f32[4,192,256]{2,1,0:T(8,128)S(1)}, u32[]{:S(2)}, u32[]{:S(2)}) %collective-permute-start.3) | collective-permute-done | bytes 786464 | tf_op jit(solution)/shard_map/ppermute | solution.py:452
  105.5 20.0 %shard_map.77 = (f32[1536,256]{1,0:T(8,128)}, f32[768,256]{1,0:T(8,128)}, bf16[768,256]{1,0:T(8,128)(2,1)}) custom-call(s32[2]{0:T(128)} %pad_add_fusion.refs_0_, f32[4,192,256]{2,1,0:T(8,128)} %copy-done.15, f32[4,192,256]{2,1,0:T(8,128)} %copy-done.27, f32[768,1536]{1,0:T(8,128)} %bitcast.49, f32[1024,4096]{1,0:T(8,128)} %get-tuple-element.17.refs_4_.refs_2_), custom_call_target="tpu_custom_call" | custom-call | flops 12800000000 | bytes 5898240 | tf_op jit(solution)/shard_map/pallas_call | solution.py:261
  127.0 4.1 all-gather.16.cloned.1.call-done
  133.2 32.0 %shard_map.78.refs_6_.total = f32[1024,4096]{1,0:T(8,128)} custom-call(s32[1]{0:T(128)} %constant.103.clone.1.first, f32[768,3072]{1,0:T(8,128)} %collective-permute-done.5.values, s32[1,1,768]{2,1,0:T(1,128)} %get-tuple-element.46.refs_0_.other_links, s32[4,1,1,768]{3,2,1,0:T(1,128)} %get-tuple-element.48.refs_1_.other_links, ...), custom_call_target="tpu_custom_call", output_to_operand_aliasing={{}: (4, {})} | custom-call | flops 22548578304 | bytes 42991616 | tf_op jit(solution)/shard_map/pallas_call | solution.py:327
  166.3 46.5 %shard_map.79 = (f32[1536,512]{1,0:T(8,128)}, f32[768,512]{1,0:T(8,128)}, bf16[768,512]{1,0:T(8,128)(2,1)}) custom-call(s32[2]{0:T(128)} %pad_add_fusion.refs_0_, f32[4,192,512]{2,1,0:T(8,128)} %bitcast.54, f32[4,192,512]{2,1,0:T(8,128)} %copy-done.23, f32[1536,256]{1,0:T(8,128)} %get-tuple-element.18.refs_3_, f32[768,256]{1,0:T(8,128)} %get-tuple-element.19.refs_4_, ...), custom_call_target="tpu_custom_call" | custom-call | flops 25600000000 | bytes 11796480 | tf_op jit(solution)/shard_map/pallas_call | solution.py:261
  214.3 22.4 %all-gather.3 = f32[768,256]{1,0:T(8,128)S(1)} all-gather(f32[192,256]{1,0:T(8,128)S(1)} %get-tuple-element.42), channel_id=5, replica_groups=mesh['leaf'=4,'prow'=4,'pcol'=2] {'prow'}, dimensions={0}, use_global_device_ids=true | all-gather | bytes 983040 | tf_op jit(solution)/shard_map/all_gather | solution.py:481
  237.4 2.7 constant_dynamic-slice_fusion.6
  241.0 43.6 %shard_map.80 = (f32[768,512]{1,0:T(8,128)}, f32[768,512]{1,0:T(8,128)}, bf16[768,512]{1,0:T(8,128)(2,1)}) custom-call(s32[2]{0:T(128)} %pad_add_fusion.refs_0_, f32[2,192,512]{2,1,0:T(8,128)} %bitcast.39, f32[2,192,512]{2,1,0:T(8,128)} %copy-done.24, f32[1536,256]{1,0:T(8,128)} %get-tuple-element.18.refs_3_, f32[768,256]{1,0:T(8,128)} %get-tuple-element.19.refs_4_, ...), custom_call_target="tpu_custom_call" | custom-call | flops 25600000000 | bytes 7864320 | tf_op jit(solution)/shard_map/pallas_call | solution.py:261
  284.6 4.4 collective-permute-start.23
  294.0 3.2 shard_map.85.rows
  299.7 14.5 %shard_map.86.total = f32[1024,4096]{1,0:T(8,128)} custom-call(s32[2]{0:T(128)} %fusion.places, bf16[1024,512]{1,0:T(8,128)(2,1)} %shard_map.85.rows, bf16[2,768,256]{2,1,0:T(8,128)(2,1)} %get-tuple-element.38.refs_8_.own, bf16[2,768,256]{2,1,0:T(8,128)(2,1)} %collective-permute-done.23.other, ...), custom_call_target="tpu_custom_call", output_to_operand_aliasing={{}: (6, {})} | custom-call | flops 3758096384 | bytes 16777216 | tf_op jit(solution)/shard_map/pallas_call | solution.py:399
  314.2 15.5 %collective-permute-done.22.other = bf16[2,768,256]{2,1,0:T(8,128)(2,1)S(1)} collective-permute-done((bf16[2,768,256]{2,1,0:T(8,128)(2,1)}, bf16[2,768,256]{2,1,0:T(8,128)(2,1)S(1)}, u32[]{:S(2)}, u32[]{:S(2)}) %collective-permute-start.22) | collective-permute-done | bytes 786464 | tf_op jit(solution)/shard_map/ppermute | solution.py:452
  330.5 14.0 %shard_map.87.total = f32[1024,4096]{1,0:T(8,128)} custom-call(s32[2]{0:T(128)} %fusion.1.places, bf16[1024,512]{1,0:T(8,128)(2,1)} %shard_map.85.rows, bf16[2,768,256]{2,1,0:T(8,128)(2,1)} %copy-done.17, bf16[2,768,256]{2,1,0:T(8,128)(2,1)} %copy-done.19, s32[4,1,1,768]{3,2,1,0:T(1,128)} %get-tuple-element.49.refs_2_.own_links, ...), custom_call_target="tpu_custom_call", output_to_operand_aliasing={{}: (6, {})} | custom-call | flops 3758096384 | bytes 16777216 | tf_op jit(solution)/shard_map/pallas_call | solution.py:399
  345.5 4.5 shard_map.84.rows
  350.8 4.6 shard_map.83.rows
  355.4 3.3 constant_dynamic-slice_fusion.4
  360.6 23.5 %shard_map.81 = (f32[384,256]{1,0:T(8,128)}, f32[768,256]{1,0:T(8,128)}, bf16[768,256]{1,0:T(8,128)(2,1)}) custom-call(s32[2]{0:T(128)} %pad_add_fusion.refs_0_, f32[1,192,256]{2,1,0:T(8,128)} %slice_bitcast_fusion.refs_10_.refs_1_, f32[1,192,256]{2,1,0:T(8,128)} %collective-permute-done.7.refs_2_, f32[1536,256]{1,0:T(8,128)} %get-tuple-element.18.refs_3_, ...), custom_call_target="tpu_custom_call" | custom-call | flops 12800000000 | bytes 2949120 | tf_op jit(solution)/shard_map/pallas_call | solution.py:261
  384.5 3.5 constant_dynamic-slice_fusion
  390.6 2.6 maximum_bitcast_fusion
  393.7 3.1 shard_map.82.rows
  397.9 17.5 %shard_map.88.total = f32[1024,4096]{1,0:T(8,128)} custom-call(s32[2]{0:T(128)} %fusion.places, bf16[1024,1024]{1,0:T(8,128)(2,1)} %shard_map.84.rows, bf16[2,768,512]{2,1,0:T(8,128)(2,1)} %copy-done, bf16[2,768,512]{2,1,0:T(8,128)(2,1)} %collective-permute-done.19.other, ...), custom_call_target="tpu_custom_call", output_to_operand_aliasing={{}: (6, {})} | custom-call | flops 7516192768 | bytes 16777216 | tf_op jit(solution)/shard_map/pallas_call | solution.py:399
  415.5 13.9 %collective-permute-done.17.own = bf16[2,768,512]{2,1,0:T(8,128)(2,1)} collective-permute-done((bf16[2,768,512]{2,1,0:T(8,128)(2,1)S(1)}, bf16[2,768,512]{2,1,0:T(8,128)(2,1)}, u32[]{:S(2)}, u32[]{:S(2)}) %collective-permute-start.17) | collective-permute-done | bytes 1572896 | tf_op jit(solution)/shard_map/ppermute | solution.py:452
  429.4 17.3 %shard_map.89.total = f32[1024,4096]{1,0:T(8,128)} custom-call(s32[2]{0:T(128)} %fusion.1.places, bf16[1024,1024]{1,0:T(8,128)(2,1)} %shard_map.84.rows, bf16[2,768,512]{2,1,0:T(8,128)(2,1)} %collective-permute-done.17.own, bf16[2,768,512]{2,1,0:T(8,128)(2,1)} %collective-permute-done.18.other, ...), custom_call_target="tpu_custom_call", output_to_operand_aliasing={{}: (6, {})} | custom-call | flops 7516192768 | bytes 16777216 | tf_op jit(solution)/shard_map/pallas_call | solution.py:399
  449.0 17.3 %shard_map.90.total = f32[1024,4096]{1,0:T(8,128)} custom-call(s32[2]{0:T(128)} %fusion.places, bf16[1024,1024]{1,0:T(8,128)(2,1)} %shard_map.83.rows, bf16[2,768,512]{2,1,0:T(8,128)(2,1)} %copy-done.1, bf16[2,768,512]{2,1,0:T(8,128)(2,1)} %collective-permute-done.15.other, ...), custom_call_target="tpu_custom_call", output_to_operand_aliasing={{}: (6, {})} | custom-call | flops 7516192768 | bytes 16777216 | tf_op jit(solution)/shard_map/pallas_call | solution.py:399
  467.7 29.1 %collective-permute-done.13.own = bf16[2,768,512]{2,1,0:T(8,128)(2,1)} collective-permute-done((bf16[2,768,512]{2,1,0:T(8,128)(2,1)S(1)}, bf16[2,768,512]{2,1,0:T(8,128)(2,1)}, u32[]{:S(2)}, u32[]{:S(2)}) %collective-permute-start.13) | collective-permute-done | bytes 1572896 | tf_op jit(solution)/shard_map/ppermute | solution.py:452
  496.8 17.3 %shard_map.91.total = f32[1024,4096]{1,0:T(8,128)} custom-call(s32[2]{0:T(128)} %fusion.1.places, bf16[1024,1024]{1,0:T(8,128)(2,1)} %shard_map.83.rows, bf16[2,768,512]{2,1,0:T(8,128)(2,1)} %collective-permute-done.13.own, bf16[2,768,512]{2,1,0:T(8,128)(2,1)} %collective-permute-done.14.other, ...), custom_call_target="tpu_custom_call", output_to_operand_aliasing={{}: (6, {})} | custom-call | flops 7516192768 | bytes 16777216 | tf_op jit(solution)/shard_map/pallas_call | solution.py:399
  515.0 14.0 %shard_map.92.total = f32[1024,4096]{1,0:T(8,128)} custom-call(s32[2]{0:T(128)} %fusion.places, bf16[1024,512]{1,0:T(8,128)(2,1)} %shard_map.82.rows, bf16[2,768,256]{2,1,0:T(8,128)(2,1)} %copy-done.3, bf16[2,768,256]{2,1,0:T(8,128)(2,1)} %copy-done.20, s32[4,1,1,768]{3,2,1,0:T(1,128)} %get-tuple-element.49.refs_2_.own_links, ...), custom_call_target="tpu_custom_call", output_to_operand_aliasing={{}: (6, {})} | custom-call | flops 3758096384 | bytes 16777216 | tf_op jit(solution)/shard_map/pallas_call | solution.py:399
  531.3 14.0 %shard_map.93 = f32[1024,4096]{1,0:T(8,128)} custom-call(s32[2]{0:T(128)} %fusion.1.places, bf16[1024,512]{1,0:T(8,128)(2,1)} %shard_map.82.rows, bf16[2,768,256]{2,1,0:T(8,128)(2,1)} %copy-done.18, bf16[2,768,256]{2,1,0:T(8,128)(2,1)} %copy-done.16, s32[4,1,1,768]{3,2,1,0:T(1,128)} %get-tuple-element.49.refs_2_.own_links, ...), custom_call_target="tpu_custom_call", output_to_operand_aliasing={{}: (6, {})} | custom-call | flops 3758096384 | bytes 16777216 | tf_op jit(solution)/shard_map/pallas_call | solution.py:399
  (131 shorter events, 43.3 us)
Async XLA Ops:
  7.2 118.6 %all-gather.14.cloned.1.call-start = ((), (), s32[]{:S(2)}) async-start(), calls=%async_computation | async-start | bytes 1966080 | tf_op jit(solution)/shard_map/all_gather | solution.py:481
  45.1 88.1 %collective-permute-start.5 = (f32[768,3072]{1,0:T(8,128)}, f32[768,3072]{1,0:T(8,128)}, u32[]{:S(2)}, u32[]{:S(2)}) collective-permute-start(f32[768,3072]{1,0:T(8,128)} %get-tuple-element.20), channel_id=1, source_target_pairs={{0,8},{8,0},{16,24},{24,16},{1,9},{9,1},{17,25},{25,17},{2,10},{10... | collective-permute-start | bytes 28311560 | tf_op jit(solution)/shard_map/ppermute | solution.py:443
  46.7 84.4 %all-gather.16.cloned.1.call-start = ((), (), s32[]{:S(2)}) async-start(), calls=%async_computation.1 | async-start | bytes 1966080 | tf_op jit(solution)/shard_map/all_gather | solution.py:481
  47.5 189.9 %all-gather.18.cloned.1.call-start = ((), (), s32[]{:S(2)}) async-start(), calls=%async_computation.2 | async-start | bytes 1966080 | tf_op jit(solution)/shard_map/all_gather | solution.py:506
  47.6 6.6 %collective-permute-start = (f32[192,256]{1,0:T(8,128)S(1)}, f32[192,256]{1,0:T(8,128)S(1)}, u32[]{:S(2)}, u32[]{:S(2)}) collective-permute-start(f32[192,256]{1,0:T(8,128)S(1)} %get-tuple-element.43), channel_id=1, source_target_pairs={{0,2},{2,4},{4,6},{6,0},{1,3},{3,5},{5,7},{7,1},{8,10},{10,12},{12... | collective-permute-start | bytes 589832 | tf_op jit(solution)/shard_map/ppermute | solution.py:473
  48.9 28.2 %collective-permute-start.1 = (f32[192,256]{1,0:T(8,128)S(1)}, f32[192,256]{1,0:T(8,128)S(1)}, u32[]{:S(2)}, u32[]{:S(2)}) collective-permute-start(f32[192,256]{1,0:T(8,128)S(1)} %get-tuple-element.43), channel_id=1, source_target_pairs={{0,4},{2,6},{4,0},{6,2},{1,5},{3,7},{5,1},{7,3},{8,12},{10,14},{12... | collective-permute-start | bytes 589832 | tf_op jit(solution)/shard_map/ppermute | solution.py:473
  50.0 35.8 %collective-permute-start.2 = (f32[192,256]{1,0:T(8,128)S(1)}, f32[192,256]{1,0:T(8,128)S(1)}, u32[]{:S(2)}, u32[]{:S(2)}) collective-permute-start(f32[192,256]{1,0:T(8,128)S(1)} %get-tuple-element.43), channel_id=1, source_target_pairs={{0,6},{2,0},{4,2},{6,4},{1,7},{3,1},{5,3},{7,5},{8,14},{10,8},{12,... | collective-permute-start | bytes 589832 | tf_op jit(solution)/shard_map/ppermute | solution.py:473
  85.9 18.7 %collective-permute-start.3 = (f32[4,192,256]{2,1,0:T(8,128)S(1)}, f32[4,192,256]{2,1,0:T(8,128)S(1)}, u32[]{:S(2)}, u32[]{:S(2)}) collective-permute-start(f32[4,192,256]{2,1,0:T(8,128)S(1)} %pad_maximum_fusion.refs_1_), channel_id=1, source_target_pairs={{0,1},{1,0},{2,3},{3,2},{4,5},{5,4},{6,7},{7,6},{8,9},{9,8},{10,11... | collective-permute-start | bytes 2359304 | tf_op jit(solution)/shard_map/ppermute | solution.py:452
  125.5 229.9 %all-gather.20.cloned.1.call-start = ((), (), s32[]{:S(2)}) async-start(), calls=%async_computation.3 | async-start | bytes 3932160 | tf_op jit(solution)/shard_map/all_gather | solution.py:506
  125.7 39.4 %collective-permute-start.4 = (f32[4,192,512]{2,1,0:T(8,128)}, f32[4,192,512]{2,1,0:T(8,128)S(1)}, u32[]{:S(2)}, u32[]{:S(2)}) collective-permute-start(f32[4,192,512]{2,1,0:T(8,128)} %bitcast.53), channel_id=1, source_target_pairs={{0,1},{1,0},{2,3},{3,2},{4,5},{5,4},{6,7},{7,6},{8,9},{9,8},{10,11... | collective-permute-start | bytes 4718600 | tf_op jit(solution)/shard_map/ppermute | solution.py:452
  212.9 171.6 %all-gather.24.cloned.1.call-start = ((), (), s32[]{:S(2)}) async-start(), calls=%async_computation.5 | async-start | bytes 3932160 | tf_op jit(solution)/shard_map/all_gather | solution.py:506
  212.9 27.1 %collective-permute-start.6 = (f32[2,192,512]{2,1,0:T(8,128)S(1)}, f32[2,192,512]{2,1,0:T(8,128)S(1)}, u32[]{:S(2)}, u32[]{:S(2)}) collective-permute-start(f32[2,192,512]{2,1,0:T(8,128)S(1)} %bitcast.40), channel_id=1, source_target_pairs={{0,1},{1,0},{2,3},{3,2},{4,5},{5,4},{6,7},{7,6},{8,9},{9,8},{10,11... | collective-permute-start | bytes 2359304 | tf_op jit(solution)/shard_map/ppermute | solution.py:452
  241.0 48.1 %copy-start.21 = (bf16[768,256]{1,0:T(8,128)(2,1)S(1)}, bf16[768,256]{1,0:T(8,128)(2,1)}, u32[]{:S(2)}) copy-start(bf16[768,256]{1,0:T(8,128)(2,1)} %get-tuple-element.23.own) | copy-start | bytes 1179652
  241.0 49.3 %copy-start.2 = (bf16[2,768,256]{2,1,0:T(8,128)(2,1)S(1)}, bf16[2,768,256]{2,1,0:T(8,128)(2,1)}, u32[]{:S(2)}) copy-start(bf16[2,768,256]{2,1,0:T(8,128)(2,1)} %get-tuple-element.38.refs_8_.own) | copy-start | bytes 2359300
  284.5 162.1 %all-gather.22.cloned.1.call-start = ((), (), s32[]{:S(2)}) async-start(), calls=%async_computation.4 | async-start | bytes 1966080 | tf_op jit(solution)/shard_map/all_gather | solution.py:506
  284.6 14.8 %collective-permute-start.23 = (bf16[2,768,256]{2,1,0:T(8,128)(2,1)}, bf16[2,768,256]{2,1,0:T(8,128)(2,1)}, u32[]{:S(2)}, u32[]{:S(2)}) collective-permute-start(bf16[2,768,256]{2,1,0:T(8,128)(2,1)} %get-tuple-element.37.refs_9_), channel_id=1, source_target_pairs={{0,8},{1,9},{2,10},{3,11},{4,12},{5,13},{6,14},{7,15},{8,0},{9,1},... | collective-permute-start | bytes 2359304 | tf_op jit(solution)/shard_map/ppermute | solution.py:452
  289.0 4.9 collective-permute-start.20
  289.1 71.5 %collective-permute-start.7 = (f32[1,192,256]{2,1,0:T(8,128)}, f32[1,192,256]{2,1,0:T(8,128)}, u32[]{:S(2)}, u32[]{:S(2)}) collective-permute-start(f32[1,192,256]{2,1,0:T(8,128)} %slice_bitcast_fusion.refs_10_.refs_1_), channel_id=1, source_target_pairs={{0,1},{1,0},{2,3},{3,2},{4,5},{5,4},{6,7},{7,6},{8,9},{9,8},{10,11... | collective-permute-start | bytes 589832 | tf_op jit(solution)/shard_map/ppermute | solution.py:452
  290.3 23.9 %collective-permute-start.21 = (bf16[2,768,256]{2,1,0:T(8,128)(2,1)S(1)}, bf16[2,768,256]{2,1,0:T(8,128)(2,1)S(1)}, u32[]{:S(2)}, u32[]{:S(2)}) collective-permute-start(bf16[2,768,256]{2,1,0:T(8,128)(2,1)S(1)} %copy-done.2), channel_id=1, source_target_pairs={{0,1},{1,0},{2,3},{3,2},{4,5},{5,4},{6,7},{7,6},{8,9},{9,8},{10,11... | collective-permute-start | bytes 2359304 | tf_op jit(solution)/shard_map/ppermute | solution.py:452
  291.7 37.9 %collective-permute-start.22 = (bf16[2,768,256]{2,1,0:T(8,128)(2,1)}, bf16[2,768,256]{2,1,0:T(8,128)(2,1)S(1)}, u32[]{:S(2)}, u32[]{:S(2)}) collective-permute-start(bf16[2,768,256]{2,1,0:T(8,128)(2,1)} %get-tuple-element.37.refs_9_), channel_id=1, source_target_pairs={{0,9},{1,8},{2,11},{3,10},{4,13},{5,12},{6,15},{7,14},{8,1},{9,0},... | collective-permute-start | bytes 2359304 | tf_op jit(solution)/shard_map/ppermute | solution.py:452
  297.2 47.4 %collective-permute-start.16 = (bf16[768,512]{1,0:T(8,128)(2,1)S(1)}, bf16[768,512]{1,0:T(8,128)(2,1)S(1)}, u32[]{:S(2)}, u32[]{:S(2)}) collective-permute-start(bf16[768,512]{1,0:T(8,128)(2,1)S(1)} %copy-done.12), channel_id=1, source_target_pairs={{0,8},{8,0},{16,24},{24,16},{1,9},{9,1},{17,25},{25,17},{2,10},{10... | collective-permute-start | bytes 2359304 | tf_op jit(solution)/shard_map/ppermute | solution.py:443
  299.4 50.5 %collective-permute-start.12 = (bf16[768,512]{1,0:T(8,128)(2,1)S(1)}, bf16[768,512]{1,0:T(8,128)(2,1)S(1)}, u32[]{:S(2)}, u32[]{:S(2)}) collective-permute-start(bf16[768,512]{1,0:T(8,128)(2,1)S(1)} %copy-done.13), channel_id=1, source_target_pairs={{0,8},{8,0},{16,24},{24,16},{1,9},{9,1},{17,25},{25,17},{2,10},{10... | collective-permute-start | bytes 2359304 | tf_op jit(solution)/shard_map/ppermute | solution.py:443
  358.7 38.1 %collective-permute-start.19 = (bf16[2,768,512]{2,1,0:T(8,128)(2,1)}, bf16[2,768,512]{2,1,0:T(8,128)(2,1)}, u32[]{:S(2)}, u32[]{:S(2)}) collective-permute-start(bf16[2,768,512]{2,1,0:T(8,128)(2,1)} %get-tuple-element.33.refs_11_), channel_id=1, source_target_pairs={{0,8},{1,9},{2,10},{3,11},{4,12},{5,13},{6,14},{7,15},{8,0},{9,1},... | collective-permute-start | bytes 4718600 | tf_op jit(solution)/shard_map/ppermute | solution.py:452
  358.7 70.6 %collective-permute-start.18 = (bf16[2,768,512]{2,1,0:T(8,128)(2,1)}, bf16[2,768,512]{2,1,0:T(8,128)(2,1)}, u32[]{:S(2)}, u32[]{:S(2)}) collective-permute-start(bf16[2,768,512]{2,1,0:T(8,128)(2,1)} %get-tuple-element.33.refs_11_), channel_id=1, source_target_pairs={{0,9},{1,8},{2,11},{3,10},{4,13},{5,12},{6,15},{7,14},{8,1},{9,0},... | collective-permute-start | bytes 4718600 | tf_op jit(solution)/shard_map/ppermute | solution.py:452
  359.5 69.9 %collective-permute-start.17 = (bf16[2,768,512]{2,1,0:T(8,128)(2,1)S(1)}, bf16[2,768,512]{2,1,0:T(8,128)(2,1)}, u32[]{:S(2)}, u32[]{:S(2)}) collective-permute-start(bf16[2,768,512]{2,1,0:T(8,128)(2,1)S(1)} %get-tuple-element.34.refs_10_.own), channel_id=1, source_target_pairs={{0,1},{1,0},{2,3},{3,2},{4,5},{5,4},{6,7},{7,6},{8,9},{9,8},{10,11... | collective-permute-start | bytes 4718600 | tf_op jit(solution)/shard_map/ppermute | solution.py:452
  384.1 9.1 %collective-permute-start.8 = (bf16[768,256]{1,0:T(8,128)(2,1)}, bf16[768,256]{1,0:T(8,128)(2,1)}, u32[]{:S(2)}, u32[]{:S(2)}) collective-permute-start(bf16[768,256]{1,0:T(8,128)(2,1)} %get-tuple-element.29.own), channel_id=1, source_target_pairs={{0,8},{8,0},{16,24},{24,16},{1,9},{9,1},{17,25},{25,17},{2,10},{10... | collective-permute-start | bytes 1179656 | tf_op jit(solution)/shard_map/ppermute | solution.py:443
  388.0 61.0 %collective-permute-start.15 = (bf16[2,768,512]{2,1,0:T(8,128)(2,1)}, bf16[2,768,512]{2,1,0:T(8,128)(2,1)}, u32[]{:S(2)}, u32[]{:S(2)}) collective-permute-start(bf16[2,768,512]{2,1,0:T(8,128)(2,1)} %get-tuple-element.31), channel_id=1, source_target_pairs={{0,8},{1,9},{2,10},{3,11},{4,12},{5,13},{6,14},{7,15},{8,0},{9,1},... | collective-permute-start | bytes 4718600 | tf_op jit(solution)/shard_map/ppermute | solution.py:452
  393.2 103.6 %collective-permute-start.14 = (bf16[2,768,512]{2,1,0:T(8,128)(2,1)}, bf16[2,768,512]{2,1,0:T(8,128)(2,1)}, u32[]{:S(2)}, u32[]{:S(2)}) collective-permute-start(bf16[2,768,512]{2,1,0:T(8,128)(2,1)} %get-tuple-element.31), channel_id=1, source_target_pairs={{0,9},{1,8},{2,11},{3,10},{4,13},{5,12},{6,15},{7,14},{8,1},{9,0},... | collective-permute-start | bytes 4718600 | tf_op jit(solution)/shard_map/ppermute | solution.py:452
  396.9 99.9 %collective-permute-start.13 = (bf16[2,768,512]{2,1,0:T(8,128)(2,1)S(1)}, bf16[2,768,512]{2,1,0:T(8,128)(2,1)}, u32[]{:S(2)}, u32[]{:S(2)}) collective-permute-start(bf16[2,768,512]{2,1,0:T(8,128)(2,1)S(1)} %get-tuple-element.32.own), channel_id=1, source_target_pairs={{0,1},{1,0},{2,3},{3,2},{4,5},{5,4},{6,7},{7,6},{8,9},{9,8},{10,11... | collective-permute-start | bytes 4718600 | tf_op jit(solution)/shard_map/ppermute | solution.py:452
  448.2 65.9 %collective-permute-start.11 = (bf16[2,768,256]{2,1,0:T(8,128)(2,1)S(1)}, bf16[2,768,256]{2,1,0:T(8,128)(2,1)S(1)}, u32[]{:S(2)}, u32[]{:S(2)}) collective-permute-start(bf16[2,768,256]{2,1,0:T(8,128)(2,1)S(1)} %get-tuple-element.35), channel_id=1, source_target_pairs={{0,8},{1,9},{2,10},{3,11},{4,12},{5,13},{6,14},{7,15},{8,0},{9,1},... | collective-permute-start | bytes 2359304 | tf_op jit(solution)/shard_map/ppermute | solution.py:452
  466.3 62.7 %collective-permute-start.10 = (bf16[2,768,256]{2,1,0:T(8,128)(2,1)S(1)}, bf16[2,768,256]{2,1,0:T(8,128)(2,1)S(1)}, u32[]{:S(2)}, u32[]{:S(2)}) collective-permute-start(bf16[2,768,256]{2,1,0:T(8,128)(2,1)S(1)} %get-tuple-element.35), channel_id=1, source_target_pairs={{0,9},{1,8},{2,11},{3,10},{4,13},{5,12},{6,15},{7,14},{8,1},{9,0},... | collective-permute-start | bytes 2359304 | tf_op jit(solution)/shard_map/ppermute | solution.py:452
  466.6 63.7 %collective-permute-start.9 = (bf16[2,768,256]{2,1,0:T(8,128)(2,1)S(1)}, bf16[2,768,256]{2,1,0:T(8,128)(2,1)S(1)}, u32[]{:S(2)}, u32[]{:S(2)}) collective-permute-start(bf16[2,768,256]{2,1,0:T(8,128)(2,1)S(1)} %get-tuple-element.36.own), channel_id=1, source_target_pairs={{0,1},{1,0},{2,3},{3,2},{4,5},{5,4},{6,7},{7,6},{8,9},{9,8},{10,11... | collective-permute-start | bytes 2359304 | tf_op jit(solution)/shard_map/ppermute | solution.py:452
  (26 other events, 190.3 us)
Sparse Core Ops, SparseCore 0:
  46.8 45.3 all-gather.13
  93.8 37.2 all-gather.15
  132.7 36.0 all-gather.17
  213.0 69.9 all-gather.19
  284.7 65.2 all-gather.23
  384.6 36.2 all-gather.21
